TPU v7x, 128 devices: a whole 4x4x4 slice. The times are simulated.
128 devices in a mesh: ctx: 32 (over z, y_hi, x), ch: 4 (over y_lo, core).
Axes of the slice: x: 4, y: 4 (y_hi: 2, y_lo: 2; y = y_hi * 2 + y_lo), z: 4, core: 2. Of those that a mesh axis runs over, the one named last changes fastest.
Arguments:
- features: bfloat16 [24576, 8192], P('ctx', 'ch'), may hold values from -6 to 6
- in_weight: bfloat16 [8192, 3, 1024], P(None, None, 'ch'), may hold values from -0.0625 to 0.0625
- filter_taps: bfloat16 [1536, 1024], P('ctx', 'ch'), may hold values from -0.15625 to 0.15625
Outputs:
- gated: bfloat16 [24576, 1024], P('ctx', 'ch')
All inputs are finite; a program needn't handle non-finite values.
Results may differ from a plain program's by a relative error of at most 0.012.
Values may be sent and summed in bfloat16 or wider, within the bound.
No kernel may reach another device: no remote copies, remote signals or barrier semaphores. Data moves between devices by JAX's collectives and lax.ppermute only.
A program may use at most 128 MiB of HBM per device.

v0:
```python
import jax
import jax.numpy as jnp
from jax import lax
from jax.sharding import PartitionSpec as P


def shifted(shard, axis, by):
    peers = lax.axis_size(axis)
    pairs = [(i, i + by) for i in range(peers) if 0 <= i + by < peers]
    return lax.ppermute(shard, axis, pairs)


def body(features, in_weight, filter_taps):
    row_count = features.shape[0]
    slab_width = in_weight.shape[2]
    full_width = in_weight.shape[0]
    flat_weight = in_weight.reshape(full_width, 3 * slab_width)
    projected = jnp.dot(
        lax.all_gather(features, "ch", axis=1, tiled=True),
        flat_weight,
        preferred_element_type=jnp.float32,
    )
    projected = projected.reshape(row_count, 3, slab_width)
    queries = projected[:, 0, :].astype(jnp.bfloat16)
    product = (projected[:, 1, :] * projected[:, 2, :]).astype(jnp.bfloat16)
    carried = product
    received = []
    for repeat in range(2):
        carried = shifted(carried, "ctx", 1)
        received.append(carried)
    previous = received[0]
    older_span = received[1]
    all_taps = lax.all_gather(filter_taps, "ctx", axis=0, tiled=True)
    block_size = min(128, row_count)
    block_count = row_count // block_size
    lag_total = all_taps.shape[0]
    turn_count = lag_total // block_size + 1
    sources = jnp.concatenate([older_span, previous, product], 0).reshape(
        3 * block_count, block_size, slab_width
    )
    edge_zeros = jnp.zeros((block_size, slab_width), jnp.bfloat16)
    padded_taps = jnp.concatenate([edge_zeros, all_taps, edge_zeros], 0).T
    row_index = lax.broadcasted_iota(jnp.int32, (block_size, block_size), 0)
    col_index = lax.broadcasted_iota(jnp.int32, (block_size, block_size), 1)
    offsets = block_size + row_index - col_index

    def lag_step(summed, lag_block):
        window = lax.dynamic_slice_in_dim(padded_taps, lag_block * block_size, 2 * block_size, 1)
        matrix = window[:, offsets]
        source_blocks = lax.dynamic_slice_in_dim(
            sources, 2 * block_count - lag_block, block_count, 0
        )
        return (
            summed
            + jnp.einsum("dab,nbd->nad", matrix, source_blocks, preferred_element_type=jnp.float32),
            None,
        )

    summed, unused = lax.scan(
        lag_step,
        jnp.zeros((block_count, block_size, slab_width), jnp.float32),
        jnp.arange(turn_count),
    )
    convolved = summed.reshape(row_count, slab_width)
    return (queries.astype(jnp.float32) * convolved).astype(jnp.bfloat16)


def solution(mesh):
    in_specs = (P("ctx", "ch"), P(None, None, "ch"), P("ctx", "ch"))
    out_specs = P("ctx", "ch")
    return jax.shard_map(body, mesh=mesh, in_specs=in_specs, out_specs=out_specs, check_vma=False)
```

profile of v0, /device:TPU:64, one launch (start us, length us, event | category | flops | bytes accessed | tf_op | source)
XLA Modules:
  0.0 1408.6 jit_solution(11854579559793784470)
XLA Ops:
  7.3 16.9 %copy.8 = bf16[8192,3,256]{0,2,1:T(8,128)(2,1)} copy(bf16[8192,3,256]{2,0,1:T(8,128)(2,1)} %param.6) | data formatting | bytes 25165824 | tf_op args[1]
  24.2 101.1 %all-gather.2.cloned.1.call-done = bf16[768,8192]{1,0:T(8,128)(2,1)} async-done(((bf16[768,2048]{1,0:T(8,128)(2,1)}), bf16[768,8192]{1,0:T(8,128)(2,1)}) %all-gather.2.cloned.1.call-update) | async-done | bytes 12582928 | tf_op jit(solution)/shard_map/all_gather | solution.py:19
  125.3 14.8 %fusion.12 = f32[768,3,256]{2,0,1:T(8,128)S(1)} fusion(bf16[8192,3,256]{0,2,1:T(8,128)(2,1)} %copy.8, bf16[768,8192]{1,0:T(8,128)(2,1)} %all-gather.2.cloned.1.call-done), kind=kOutput, calls=%fused_computation.11 | convolution fusion | flops 9663676416 | bytes 27525120 | tf_op jit(solution)/shard_map/dot_general | solution.py:18
  140.1 3.4 collective-permute-start
  143.5 14.0 collective-permute-done
  157.5 1.9 collective-permute-start.1
  159.4 89.7 %all_gather.7 = bf16[1536,256]{1,0:T(8,128)(2,1)S(1)} all-gather(bf16[48,256]{1,0:T(8,128)(2,1)S(1)} %copy-done.2), channel_id=1, replica_groups=mesh['ctx'=32,'ch'=4] {'ctx'}, dimensions={0}, use_global_device_ids=true | all-gather | bytes 811008 | tf_op jit(solution)/shard_map/all_gather | solution.py:33
  251.4 1148.0 %while.13 = (s32[]{:T(128)}, f32[6,128,256]{1,0,2:T(8,128)S(1)}, s32[13]{0:T(128)S(1)}, bf16[18,128,256]{2,1,0:T(8,128)(2,1)S(1)}, bf16[256,1792]{0,1:T(8,128)(2...) while((s32[]{:T(128)}, f32[6,128,256]{1,0,2:T(8,128)S(1)}, ...), condition=%wide.region_1.2_spmd.clone, body=%wide.region_0.1_spmd.clone.sunk | while | flops 50806792 | bytes 45875948 | solution.py:59
  253.7 65.2 %gather_fusion = bf16[16384,256]{1,0:T(8,128)(2,1)} fusion(bf16[256,256]{0,1:T(8,128)(2,1)S(1)} %constant_dynamic-slice_fusion.5, s32[16384]{0:T(1024)S(1)} %fusion.26), kind=kCustom, calls=%fused_computation.clone.clone.1 | custom fusion | bytes 16842752 | tf_op jit(solution)/shard_map/while/body/eval_jaxpr/gather | solution.py:49
  318.9 12.4 copy.15
  333.0 6.7 fusion.27
  342.0 65.2 %gather_fusion = bf16[16384,256]{1,0:T(8,128)(2,1)} fusion(bf16[256,256]{0,1:T(8,128)(2,1)S(1)} %constant_dynamic-slice_fusion.5, s32[16384]{0:T(1024)S(1)} %fusion.26), kind=kCustom, calls=%fused_computation.clone.clone.1 | custom fusion | bytes 16842752 | tf_op jit(solution)/shard_map/while/body/eval_jaxpr/gather | solution.py:49
  407.2 12.4 copy.15
  421.3 6.7 fusion.27
  430.3 65.2 %gather_fusion = bf16[16384,256]{1,0:T(8,128)(2,1)} fusion(bf16[256,256]{0,1:T(8,128)(2,1)S(1)} %constant_dynamic-slice_fusion.5, s32[16384]{0:T(1024)S(1)} %fusion.26), kind=kCustom, calls=%fused_computation.clone.clone.1 | custom fusion | bytes 16842752 | tf_op jit(solution)/shard_map/while/body/eval_jaxpr/gather | solution.py:49
  495.5 12.4 copy.15
  509.6 6.7 fusion.27
  518.6 65.2 %gather_fusion = bf16[16384,256]{1,0:T(8,128)(2,1)} fusion(bf16[256,256]{0,1:T(8,128)(2,1)S(1)} %constant_dynamic-slice_fusion.5, s32[16384]{0:T(1024)S(1)} %fusion.26), kind=kCustom, calls=%fused_computation.clone.clone.1 | custom fusion | bytes 16842752 | tf_op jit(solution)/shard_map/while/body/eval_jaxpr/gather | solution.py:49
  583.8 12.4 copy.15
  597.9 6.7 fusion.27
  606.9 65.2 %gather_fusion = bf16[16384,256]{1,0:T(8,128)(2,1)} fusion(bf16[256,256]{0,1:T(8,128)(2,1)S(1)} %constant_dynamic-slice_fusion.5, s32[16384]{0:T(1024)S(1)} %fusion.26), kind=kCustom, calls=%fused_computation.clone.clone.1 | custom fusion | bytes 16842752 | tf_op jit(solution)/shard_map/while/body/eval_jaxpr/gather | solution.py:49
  672.2 12.4 copy.15
  686.2 6.7 fusion.27
  695.2 65.2 %gather_fusion = bf16[16384,256]{1,0:T(8,128)(2,1)} fusion(bf16[256,256]{0,1:T(8,128)(2,1)S(1)} %constant_dynamic-slice_fusion.5, s32[16384]{0:T(1024)S(1)} %fusion.26), kind=kCustom, calls=%fused_computation.clone.clone.1 | custom fusion | bytes 16842752 | tf_op jit(solution)/shard_map/while/body/eval_jaxpr/gather | solution.py:49
  760.5 12.4 copy.15
  774.5 6.7 fusion.27
  783.5 65.2 %gather_fusion = bf16[16384,256]{1,0:T(8,128)(2,1)} fusion(bf16[256,256]{0,1:T(8,128)(2,1)S(1)} %constant_dynamic-slice_fusion.5, s32[16384]{0:T(1024)S(1)} %fusion.26), kind=kCustom, calls=%fused_computation.clone.clone.1 | custom fusion | bytes 16842752 | tf_op jit(solution)/shard_map/while/body/eval_jaxpr/gather | solution.py:49
  848.8 12.4 copy.15
  862.8 6.7 fusion.27
  871.8 65.2 %gather_fusion = bf16[16384,256]{1,0:T(8,128)(2,1)} fusion(bf16[256,256]{0,1:T(8,128)(2,1)S(1)} %constant_dynamic-slice_fusion.5, s32[16384]{0:T(1024)S(1)} %fusion.26), kind=kCustom, calls=%fused_computation.clone.clone.1 | custom fusion | bytes 16842752 | tf_op jit(solution)/shard_map/while/body/eval_jaxpr/gather | solution.py:49
  937.1 12.4 copy.15
  951.1 6.7 fusion.27
  960.1 65.2 %gather_fusion = bf16[16384,256]{1,0:T(8,128)(2,1)} fusion(bf16[256,256]{0,1:T(8,128)(2,1)S(1)} %constant_dynamic-slice_fusion.5, s32[16384]{0:T(1024)S(1)} %fusion.26), kind=kCustom, calls=%fused_computation.clone.clone.1 | custom fusion | bytes 16842752 | tf_op jit(solution)/shard_map/while/body/eval_jaxpr/gather | solution.py:49
  1025.4 12.4 copy.15
  1039.4 6.7 fusion.27
  1048.4 65.2 %gather_fusion = bf16[16384,256]{1,0:T(8,128)(2,1)} fusion(bf16[256,256]{0,1:T(8,128)(2,1)S(1)} %constant_dynamic-slice_fusion.5, s32[16384]{0:T(1024)S(1)} %fusion.26), kind=kCustom, calls=%fused_computation.clone.clone.1 | custom fusion | bytes 16842752 | tf_op jit(solution)/shard_map/while/body/eval_jaxpr/gather | solution.py:49
  1113.7 12.4 copy.15
  1127.7 6.7 fusion.27
  1136.8 65.2 %gather_fusion = bf16[16384,256]{1,0:T(8,128)(2,1)} fusion(bf16[256,256]{0,1:T(8,128)(2,1)S(1)} %constant_dynamic-slice_fusion.5, s32[16384]{0:T(1024)S(1)} %fusion.26), kind=kCustom, calls=%fused_computation.clone.clone.1 | custom fusion | bytes 16842752 | tf_op jit(solution)/shard_map/while/body/eval_jaxpr/gather | solution.py:49
  1202.0 12.4 copy.15
  1216.0 6.7 fusion.27
  1225.1 65.2 %gather_fusion = bf16[16384,256]{1,0:T(8,128)(2,1)} fusion(bf16[256,256]{0,1:T(8,128)(2,1)S(1)} %constant_dynamic-slice_fusion.5, s32[16384]{0:T(1024)S(1)} %fusion.26), kind=kCustom, calls=%fused_computation.clone.clone.1 | custom fusion | bytes 16842752 | tf_op jit(solution)/shard_map/while/body/eval_jaxpr/gather | solution.py:49
  1290.3 12.4 copy.15
  1304.3 6.7 fusion.27
  1313.4 65.2 %gather_fusion = bf16[16384,256]{1,0:T(8,128)(2,1)} fusion(bf16[256,256]{0,1:T(8,128)(2,1)S(1)} %constant_dynamic-slice_fusion.5, s32[16384]{0:T(1024)S(1)} %fusion.26), kind=kCustom, calls=%fused_computation.clone.clone.1 | custom fusion | bytes 16842752 | tf_op jit(solution)/shard_map/while/body/eval_jaxpr/gather | solution.py:49
  1378.6 12.4 copy.15
  1392.7 6.7 fusion.27
  1399.7 2.0 fusion.16
  (82 shorter events, 28.8 us)
Async XLA Ops:
  6.5 118.7 %all-gather.2.cloned.1.call-start = ((), (), s32[]{:S(2)}) async-start(), calls=%async_computation | async-start | bytes 15728640 | tf_op jit(solution)/shard_map/all_gather | solution.py:19
  24.2 135.2 %copy-start.2 = (bf16[48,256]{1,0:T(8,128)(2,1)S(1)}, bf16[48,256]{1,0:T(8,128)(2,1)}, u32[]{:S(2)}) copy-start(bf16[48,256]{1,0:T(8,128)(2,1)} %param.7) | copy-start | bytes 73732
  140.0 19.4 %copy-start = (f32[768,3,256]{2,0,1:T(8,128)}, f32[768,3,256]{2,0,1:T(8,128)S(1)}, u32[]{:S(2)}) copy-start(f32[768,3,256]{2,0,1:T(8,128)S(1)} %fusion.12) | copy-start | bytes 7077892
  140.1 17.4 %collective-permute-start = (bf16[768,256]{1,0:T(8,128)(2,1)S(1)}, bf16[768,256]{1,0:T(8,128)(2,1)S(1)}, u32[]{:S(2)}, u32[]{:S(2)}) collective-permute-start(bf16[768,256]{1,0:T(8,128)(2,1)S(1)} %fusion.18), channel_id=1, source_target_pairs={{0,4},{4,8},{8,12},{12,16},{16,20},{20,24},{24,28},{28,32},{32,36}... | collective-permute-start | bytes 1179656 | tf_op jit(solution)/shard_map/ppermute | solution.py:10
  157.5 92.7 %copy-start.1 = (bf16[768,256]{1,0:T(8,128)(2,1)}, bf16[768,256]{1,0:T(8,128)(2,1)S(1)}, u32[]{:S(2)}) copy-start(bf16[768,256]{1,0:T(8,128)(2,1)S(1)} %collective-permute-done) | copy-start | bytes 1179652
  157.5 92.7 %collective-permute-start.1 = (bf16[768,256]{1,0:T(8,128)(2,1)S(1)}, bf16[768,256]{1,0:T(8,128)(2,1)}, u32[]{:S(2)}, u32[]{:S(2)}) collective-permute-start(bf16[768,256]{1,0:T(8,128)(2,1)S(1)} %collective-permute-done), channel_id=1, source_target_pairs={{0,4},{4,8},{8,12},{12,16},{16,20},{20,24},{24,28},{28,32},{32,36}... | collective-permute-start | bytes 1179656 | tf_op jit(solution)/shard_map/ppermute | solution.py:10
Sparse Core Ops, SparseCore 0:
  9.0 116.1 all-gather.1
where the time goes:
time: 1420 us; the launch traced here: 1410 us
  local copies, waits for them, and re-layouts  1050 us (74%)
  waiting for transfers between devices  116 us (8%)
  matrix products  102 us (7%)
  blocking collectives  89.7 us (6%)
  loops' own time  25.9 us (2%)
    gather x26, local copies, waits for them, and re-layouts, lag_step(): matrix = window[:, offsets]  1010 us
    all_gather x1, waiting for transfers between devices, body(): lax.all_gather(features, 'ch', axis=1, tiled=True)  101 us
    all_gather x1, blocking collectives, body(): all_taps = lax.all_gather(filter_taps, 'ctx', axis=0, tiled=True)  89.7 us
    dot_general x13, matrix products, lag_step(): jnp.einsum('dab,nbd->nad', matrix, source_blocks, preferred_element_type=...  87.7 us
  transfers between devices with their start and end apart: 3, of which 2 were waited for; matrix products, arithmetic and copies ran while one was open for 1% of the time, Pallas kernels for 0%

commit v1 on v0

v1 whole, which is shorter than its diff:
```python
import functools

import jax
import jax.numpy as jnp
import numpy as np
from jax import lax
from jax.experimental import pallas as pl
from jax.experimental.pallas import tpu as pltpu
from jax.sharding import PartitionSpec as P

BLOCK = 256
WHOLE = pl.BlockSpec(memory_space=pltpu.VMEM)
SCALAR = pl.BlockSpec(memory_space=pltpu.SMEM)
SMALL = pl.CostEstimate(flops=1024, bytes_accessed=1024, transcendentals=0)
CHUNKS = ((0, 256), (256, 256), (512, 128), (640, 128))
PEER = [(0, 2), (1, 3), (2, 0), (3, 1)]
SIBLING = [(0, 1), (1, 0), (2, 3), (3, 2)]


def spectral_tables():
    order = np.concatenate([np.arange(0, BLOCK, 2), np.arange(1, BLOCK, 2)])
    theta = np.pi * (2 * order + 1) / (2 * BLOCK)
    near = theta[:, None] * np.arange(BLOCK)[None, :]
    far = (np.arange(BLOCK) + BLOCK)[:, None] * theta[None, :]
    forward = np.concatenate([np.cos(near), np.sin(near)], 0)
    inverse = np.concatenate([np.cos(far), np.sin(far)], 1) / BLOCK
    return jnp.asarray(forward, jnp.bfloat16), jnp.asarray(inverse, jnp.bfloat16)


def weight_specs(depth, width, splits, first):
    return [
        pl.BlockSpec(
            (1, depth // splits, width),
            lambda s, o, kind=kind: (kind, o[first + s // splits] * splits + s % splits, 0),
        )
        for kind in range(3)
    ]


def project_own_kernel(order, own, sibling, *refs):
    weights, outs = refs[:3], refs[3:]
    step = pl.program_id(0)
    depth = weights[0].shape[1]
    splits = own.shape[1] // depth
    for turn in range(2 * splits):

        @pl.when(step == turn)
        def _():
            piece = (own, sibling)[turn // splits]
            columns = slice(turn % splits * depth, (turn % splits + 1) * depth)
            for kind, weight in enumerate(weights):
                at = 0
                for out in outs:
                    part = jnp.dot(
                        piece[at : at + out.shape[1], columns], weight[0], preferred_element_type=jnp.float32
                    )
                    out[kind] = part if turn == 0 else out[kind] + part
                    at += out.shape[1]


def project_own(order, features, sibling, weight):
    rows, depth = features.shape
    width = weight.shape[2]
    splits = 2
    alone = pl.BlockSpec((rows, depth), lambda s, o: (0, 0))
    return pl.pallas_call(
        project_own_kernel,
        out_shape=[jax.ShapeDtypeStruct((3, size, width), jnp.float32) for _, size in CHUNKS],
        grid_spec=pltpu.PrefetchScalarGridSpec(
            num_scalar_prefetch=1,
            grid=(2 * splits,),
            in_specs=[alone, alone] + weight_specs(depth, width, splits, 0),
            out_specs=[pl.BlockSpec((3, size, width), lambda s, o: (0, 0, 0)) for _, size in CHUNKS],
        ),
        compiler_params=pltpu.CompilerParams(vmem_limit_bytes=28 << 20),
        cost_estimate=SMALL,
        name="project_own",
    )(order, features, sibling, weight, weight, weight)


def project_peer_kernel(order, peer, peer_sibling, known, *refs):
    weights, (query, product, total) = refs[:3], refs[3:]
    step = pl.program_id(0)
    depth = weights[0].shape[1]
    splits = peer.shape[1] // depth
    for turn in range(2 * splits):

        @pl.when(step == turn)
        def _():
            piece = (peer, peer_sibling)[turn // splits]
            columns = slice(turn % splits * depth, (turn % splits + 1) * depth)
            full = []
            for kind, weight in enumerate(weights):
                part = jnp.dot(piece[:, columns], weight[0], preferred_element_type=jnp.float32)
                full.append(part + (known[kind] if turn == 0 else total[kind]))
            if turn < 2 * splits - 1:
                for kind in range(3):
                    total[kind] = full[kind]
            else:
                query[...] = full[0].astype(jnp.bfloat16)
                product[...] = (full[1] * full[2]).astype(jnp.bfloat16)


def project_peer(order, peer, peer_sibling, known, weight):
    rows, depth = peer.shape
    width = weight.shape[2]
    splits = 2
    alone = pl.BlockSpec((rows, depth), lambda s, o: (0, 0))
    out = pl.BlockSpec((rows, width), lambda s, o: (0, 0))
    return pl.pallas_call(
        project_peer_kernel,
        out_shape=[jax.ShapeDtypeStruct((rows, width), jnp.bfloat16)] * 2,
        grid_spec=pltpu.PrefetchScalarGridSpec(
            num_scalar_prefetch=1,
            grid=(2 * splits,),
            in_specs=[alone, alone, pl.BlockSpec((3, rows, width), lambda s, o: (0, 0, 0))]
            + weight_specs(depth, width, splits, 2),
            out_specs=[out, out],
            scratch_shapes=[pltpu.VMEM((3, rows, width), jnp.float32)],
        ),
        compiler_params=pltpu.CompilerParams(vmem_limit_bytes=16 << 20),
        cost_estimate=SMALL,
        name="project_peer",
    )(order, peer, peer_sibling, known, weight, weight, weight)


def taps_kernel(taps, forward, spectrum):
    for block in range(taps.shape[0] // BLOCK):
        spectrum[block] = jnp.dot(
            forward[...], taps[block * BLOCK : (block + 1) * BLOCK], preferred_element_type=jnp.float32
        )


def transform_taps(taps, forward):
    blocks, width = taps.shape[0] // BLOCK, taps.shape[1]
    return pl.pallas_call(
        taps_kernel,
        out_shape=jax.ShapeDtypeStruct((blocks, 2 * BLOCK, width), jnp.float32),
        compiler_params=pltpu.CompilerParams(vmem_limit_bytes=16 << 20),
        cost_estimate=SMALL,
        name="transform_taps",
    )(taps, forward)


def convolve_kernel(counts, *refs):
    n_source, n_query = counts
    sources = refs[:n_source]
    queries = refs[n_source : n_source + n_query]
    taps, forward, inverse, out, signal, spectrum, mixed = refs[n_source + n_query :]
    at = 0
    for source in sources:
        signal[at : at + source.shape[0]] = source[...]
        at += source.shape[0]
    n_blocks = at // BLOCK
    n_taps = taps.shape[0]
    n_out = n_blocks - n_taps
    for block in range(n_blocks):
        spectrum[block] = jnp.dot(
            forward[...], signal[block * BLOCK : (block + 1) * BLOCK], preferred_element_type=jnp.float32
        )
    half = BLOCK // 2
    rows = 8
    for sign in (0, 1):

        def mix(turn, carry):
            base = pl.multiple_of(sign * half + turn * rows, rows)
            cos_at = pl.ds(base, rows)
            sin_at = pl.ds(base + BLOCK, rows)
            pairs = []
            for pair in range(n_blocks - 1):
                near_cos, near_sin = spectrum[pair, cos_at], spectrum[pair, sin_at]
                far_cos, far_sin = spectrum[pair + 1, cos_at], spectrum[pair + 1, sin_at]
                if sign == 0:
                    pairs.append((near_cos - far_sin, near_sin + far_cos))
                else:
                    pairs.append((near_cos + far_sin, near_sin - far_cos))
            for j in range(n_out):
                cos_sum = sin_sum = None
                for i in range(n_taps):
                    c, s = pairs[n_taps - 1 + j - i]
                    hc, hs = taps[i, cos_at], taps[i, sin_at]
                    cc, ss = c * hc - s * hs, c * hs + s * hc
                    cos_sum = cc if cos_sum is None else cos_sum + cc
                    sin_sum = ss if sin_sum is None else sin_sum + ss
                mixed[j, cos_at] = cos_sum
                mixed[j, sin_at] = sin_sum
            return carry

        lax.fori_loop(0, half // rows, mix, 0)
    convolved = [
        jnp.dot(inverse[...], mixed[j].astype(jnp.bfloat16), preferred_element_type=jnp.float32) for j in range(n_out)
    ]
    at = 0
    for query in queries:
        for row in range(0, query.shape[0], 128):
            block, offset = (at + row) // BLOCK, (at + row) % BLOCK
            out[at + row : at + row + 128] = (
                query[row : row + 128].astype(jnp.float32) * convolved[block][offset : offset + 128]
            ).astype(jnp.bfloat16)
        at += query.shape[0]


def convolve(sources, queries, taps, forward, inverse):
    length = sum(s.shape[0] for s in sources)
    rows = sum(q.shape[0] for q in queries)
    width = queries[0].shape[1]
    blocks = length // BLOCK
    outs = rows // BLOCK
    return pl.pallas_call(
        functools.partial(convolve_kernel, (len(sources), len(queries))),
        out_shape=jax.ShapeDtypeStruct((rows, width), jnp.bfloat16),
        scratch_shapes=[
            pltpu.VMEM((length, width), jnp.bfloat16),
            pltpu.VMEM((blocks, 2 * BLOCK, width), jnp.float32),
            pltpu.VMEM((outs, 2 * BLOCK, width), jnp.float32),
        ],
        compiler_params=pltpu.CompilerParams(vmem_limit_bytes=20 << 20),
        cost_estimate=SMALL,
        name="convolve",
    )(*sources, *queries, taps, forward, inverse)


def pair_taps(taps):
    other = lax.ppermute(taps, "ctx", [(i, i ^ 4) for i in range(32)])
    upper = (lax.axis_index("ctx") & 4) != 0
    return jnp.where(upper, jnp.stack([other, taps]), jnp.stack([taps, other]))


def exchange_taps(both):
    _, lags, width = both.shape
    groups = [[z * 8 + y * 4 + x for z in range(4) for x in range(4)] for y in range(2)]
    copies = jnp.broadcast_to(both[None], (16, 2, lags, width))
    every = lax.all_to_all(copies, "ctx", 0, 0, axis_index_groups=groups, tiled=True)
    return every.reshape(4, 4, 2, lags, width).transpose(0, 2, 1, 3, 4).reshape(-1, width)


def body(features, in_weight, filter_taps):
    peers = lax.axis_size("ctx")
    ahead = [[(i, i + by) for i in range(peers - by)] for by in (1, 2)]
    me = lax.axis_index("ch")
    order = jnp.stack([me, me ^ 1, me ^ 2, me ^ 3]).astype(jnp.int32)
    weight = jnp.transpose(in_weight, (1, 0, 2))
    forward, inverse = spectral_tables()

    together = lax.optimization_barrier
    both = pair_taps(filter_taps)
    sibling = lax.ppermute(features, "ch", SIBLING)
    arrived = []
    for turn, (at, rows) in enumerate(CHUNKS):
        whole = features
        if turn == 1:
            whole, sibling = together((features, sibling))
        elif turn >= 2:
            whole, arrived[turn - 2] = together((features, arrived[turn - 2]))
        piece = whole[at : at + rows]
        if turn == 0:
            piece, both = together((piece, both))
        arrived.append(lax.ppermute(piece, "ch", PEER))
    taps = exchange_taps(both)
    known = list(project_own(order, features, sibling, weight))

    def send(group):
        return [lax.ppermute(group, "ctx", ahead[by]) for by in (0, 1)]

    def finish(turn, peer):
        peer_sibling = lax.ppermute(peer, "ch", SIBLING)
        return project_peer(order, peer, peer_sibling, known[turn], weight)

    peer, taps = together((arrived[0], taps))
    query_0, product_0 = finish(0, peer)
    halo_0 = send(product_0)
    peer, known[0], known[1] = together((arrived[1], known[0], known[1]))
    query_1, product_1 = finish(1, peer)
    spectrum = transform_taps(taps, forward)
    peer, product_0, halo_0[0], halo_0[1], spectrum = together(
        (arrived[2], product_0, halo_0[0], halo_0[1], spectrum)
    )
    query_2, product_2 = finish(2, peer)
    halo_1 = send(product_1)
    peer, product_1 = together((arrived[3], product_1))
    query_3, product_3 = finish(3, peer)
    halo_2 = send(jnp.concatenate([product_2, product_3], 0))
    sources = [halo_0[1], halo_1[1], halo_2[1], halo_0[0], halo_1[0], halo_2[0]]
    sources += [product_0, product_1, product_2, product_3]
    return convolve(sources, [query_0, query_1, query_2, query_3], spectrum, forward, inverse)


def solution(mesh):
    in_specs = (P("ctx", "ch"), P(None, None, "ch"), P("ctx", "ch"))
    out_specs = P("ctx", "ch")
    return jax.shard_map(body, mesh=mesh, in_specs=in_specs, out_specs=out_specs, check_vma=False)
```

time: 1420 us -> 118 us (0.08)
  local copies, waits for them, and re-layouts: 1050 us -> 10.4 us
  matrix products: 102 us -> 0 us
  waiting for transfers between devices: 116 us -> 31.6 us
  blocking collectives: 89.7 us -> 18.8 us
  Pallas kernels: 0 us -> 26.1 us
  loops' own time: 25.9 us -> 0 us
  starting transfers between devices: 5.3 us -> 29 us
    gather x26 -> x0, local copies, waits for them, and re-layouts: 1010 us -> none  [lag_step(): matrix = window[:, offsets]]
    dot_general x14 -> x0, matrix products: 102 us -> none  [the longest x13 87.7 us: lag_step(): jnp.einsum('dab,nbd->nad', matrix, source_blocks, preferred_element_type=...]
    all_gather x1 -> x0, waiting for transfers between devices: 101 us -> none  [body(): lax.all_gather(features, 'ch', axis=1, tiled=True)]
    all_gather x1 -> x0, blocking collectives: 89.7 us -> none  [body(): all_taps = lax.all_gather(filter_taps, 'ctx', axis=0, tiled=True)]
    pallas_call x0 -> x7, Pallas kernels: none -> 26.1 us  [the longest x4 13.3 us: project_peer(): pl.pallas_call(project_peer_kernel, out_shape=[jax.ShapeDtypeStruct((rows...]
    another operation x1 -> x0, loops' own time: 25.9 us -> none  [body(): lax.scan(lag_step, jnp.zeros((block_count, block_size, slab_width), jnp.f...]
    dynamic_slice x52 -> x0, local copies, waits for them, and re-layouts: 24.3 us -> none  [the longest x13 11.9 us: lag_step(): lax.dynamic_slice_in_dim(padded_taps, lag_block * block_size, 2 * block_s...]
    ppermute x2 -> x16, starting transfers between devices: 5.29 us -> 29 us  [the longest x6 21.5 us: send(): return [lax.ppermute(group, 'ctx', ahead[by]) for by in (0, 1)]]
  transfers between devices with their start and end apart: 3 -> 16, of which waited for: 2 -> 8; matrix products, arithmetic and copies ran while one was open for 1% -> 6% of each run, Pallas kernels for 0% -> 19%
where the time goes in v1:
time: 118 us; the launch traced here: 117 us
  waiting for transfers between devices  31.6 us (27%)
  starting transfers between devices  29 us (25%)
  Pallas kernels  26.1 us (22%)
  blocking collectives  18.8 us (16%)
  local copies, waits for them, and re-layouts  10.4 us (9%)
    ppermute x6, starting transfers between devices, send(): return [lax.ppermute(group, 'ctx', ahead[by]) for by in (0, 1)]  21.5 us
    all_to_all x1, blocking collectives, exchange_taps(): lax.all_to_all(copies, 'ctx', 0, 0, axis_index_groups=groups, tiled=True)  18.8 us
    ppermute x4, waiting for transfers between devices, body(): arrived.append(lax.ppermute(piece, 'ch', PEER))  17.8 us
    ppermute x6, waiting for transfers between devices, send(): return [lax.ppermute(group, 'ctx', ahead[by]) for by in (0, 1)]  13.8 us
    pallas_call x4, Pallas kernels, project_peer(): pl.pallas_call(project_peer_kernel, out_shape=[jax.ShapeDtypeStruct((rows...  13.3 us
    pallas_call x1, Pallas kernels, project_own(): pl.pallas_call(project_own_kernel, out_shape=[jax.ShapeDtypeStruct((3, si...  8.33 us
    slice x4, local copies, waits for them, and re-layouts, body(): piece = whole[at:at + rows]  4.7 us
    unnamed x11, local copies, waits for them, and re-layouts  4.61 us
  transfers between devices with their start and end apart: 16, of which 8 were waited for; matrix products, arithmetic and copies ran while one was open for 6% of the time, Pallas kernels for 19%

profile of v1, /device:TPU:64, one launch (start us, length us, event | category | flops | bytes accessed | tf_op | source)
XLA Modules:
  0.0 117.1 jit_solution(12707319074453883602)
XLA Ops:
  0.0 0.0 collective-permute-start.4
  0.0 3.2 %collective-permute-start = (bf16[48,256]{1,0:T(8,128)(2,1)}, bf16[48,256]{1,0:T(8,128)(2,1)S(1)}, u32[]{:S(2)}, u32[]{:S(2)}) collective-permute-start(bf16[48,256]{1,0:T(8,128)(2,1)} %param.7), channel_id=1, source_target_pairs={{0,16},{4,20},{8,24},{12,28},{16,0},{20,4},{24,8},{28,12},{32,48},... | collective-permute-start | bytes 73736 | tf_op jit(solution)/shard_map/ppermute | solution.py:224
  3.2 2.3 %slice.12 = bf16[256,2048]{1,0:T(8,128)(2,1)} slice(bf16[768,2048]{1,0:T(8,128)(2,1)} %own.1), slice={[0:256], [0:2048]} | slice | bytes 2097152 | tf_op jit(solution)/shard_map/slice | solution.py:255
  5.5 0.0 collective-permute-done
  5.5 0.9 maximum_select_fusion
  6.5 1.5 %collective-permute-start.1 = (bf16[256,2048]{1,0:T(8,128)(2,1)}, bf16[256,2048]{1,0:T(8,128)(2,1)}, u32[]{:S(2)}, u32[]{:S(2)}) collective-permute-start(bf16[256,2048]{1,0:T(8,128)(2,1)} %slice.12), channel_id=1, source_target_pairs={{0,2},{1,3},{2,0},{3,1},{4,6},{5,7},{6,4},{7,5},{8,10},{9,11},{10,... | collective-permute-start | bytes 3145736 | tf_op jit(solution)/shard_map/ppermute | solution.py:258
  8.0 0.0 collective-permute-done.4.sibling
  8.0 2.3 %slice.14 = bf16[256,2048]{1,0:T(8,128)(2,1)} slice(bf16[768,2048]{1,0:T(8,128)(2,1)} %own.1), slice={[256:512], [0:2048]} | slice | bytes 2097152 | tf_op jit(solution)/shard_map/slice | solution.py:255
  10.3 0.5 collective-permute-start.7
  10.9 0.1 broadcast_in_dim.2
  11.0 18.8 %all_to_all.5 = bf16[16,2,48,256]{3,2,1,0:T(8,128)(2,1)S(1)} all-to-all(bf16[16,2,48,256]{3,2,1,0:T(8,128)(2,1)S(1)} %broadcast_in_dim.2), channel_id=1, replica_groups={{0,4,8,12,32,36,40,44,64,68,72,76,96,100,104,108},{16,20,24,28,48,52,56..., dimensions={0} | all-to-all | bytes 1572864 | tf_op jit(solution)/shard_map/all_to_all | solution.py:233
  29.8 1.0 copy.6
  30.8 2.1 %collective-permute-done.1.peer = bf16[256,2048]{1,0:T(8,128)(2,1)} collective-permute-done((bf16[256,2048]{1,0:T(8,128)(2,1)}, bf16[256,2048]{1,0:T(8,128)(2,1)}, u32[]{:S(2)}, u32[]{:S(2)}) %collective-permute-start.1) | collective-permute-done | bytes 1048608 | tf_op jit(solution)/shard_map/ppermute | solution.py:258
  32.8 0.0 collective-permute-start.3
  32.9 0.1 pad_add_fusion.order
  32.9 4.6 %copy-done = bf16[8192,3,256]{2,0,1:T(8,128)(2,1)S(1)} copy-done((bf16[8192,3,256]{2,0,1:T(8,128)(2,1)S(1)}, bf16[8192,3,256]{2,0,1:T(8,128)(2,1)}, u32[]{:S(2)}) %copy-start) | copy-done | bytes 12582936
  37.5 8.3 %project_own.1 = (f32[3,256,256]{2,1,0:T(8,128)S(1)}, f32[3,256,256]{2,1,0:T(8,128)S(1)}, f32[3,128,256]{2,1,0:T(8,128)S(1)}, f32[3,128,256]{2,1,0:T(8,128)S(1)}) custom-call(s32[4]{0:T(128)S(1)} %pad_add_fusion.order, bf16[768,2048]{1,0:T(8,128)(2,1)S(1)} %copy-done.1, bf16[768,2048]{1,0:T(8,128)(2,1)} %collective-permute-done.4.sibling, ...), custom_call_target="tpu_custom_call" | custom-call | flops 1024 | bytes 1024 | tf_op jit(solution)/shard_map/project_own/pallas_call | solution.py:66
  45.8 8.7 %collective-permute-done.7.peer = bf16[256,2048]{1,0:T(8,128)(2,1)} collective-permute-done((bf16[256,2048]{1,0:T(8,128)(2,1)}, bf16[256,2048]{1,0:T(8,128)(2,1)}, u32[]{:S(2)}, u32[]{:S(2)}) %collective-permute-start.7) | collective-permute-done | bytes 1048608 | tf_op jit(solution)/shard_map/ppermute | solution.py:258
  54.6 0.0 collective-permute-start.8
  54.6 0.8 collective-permute-start.2
  55.5 0.0 copy-start.3
  55.5 1.4 %collective-permute-start.11 = (bf16[128,2048]{1,0:T(8,128)(2,1)S(1)}, bf16[128,2048]{1,0:T(8,128)(2,1)S(1)}, u32[]{:S(2)}, u32[]{:S(2)}) collective-permute-start(bf16[128,2048]{1,0:T(8,128)(2,1)S(1)} %slice.15), channel_id=1, source_target_pairs={{0,2},{1,3},{2,0},{3,1},{4,6},{5,7},{6,4},{7,5},{8,10},{9,11},{10,... | collective-permute-start | bytes 1572872 | tf_op jit(solution)/shard_map/ppermute | solution.py:258
  56.9 0.0 collective-permute-done.3.peer_sibling
  56.9 4.6 %project_peer.4 = (bf16[256,256]{1,0:T(8,128)(2,1)S(1)}, bf16[256,256]{1,0:T(8,128)(2,1)S(1)}) custom-call(s32[4]{0:T(128)S(1)} %pad_add_fusion.order, bf16[256,2048]{1,0:T(8,128)(2,1)} %collective-permute-done.1.peer, bf16[256,2048]{1,0:T(8,128)(2,1)} %collective-permute-done.3.peer_sibling, f32[3,256,256]{2,1,0:T(8,128)S(1)} %get-tuple-element.42.known, ...), custom_call_target="tpu_custom_call" | custom-call | flops 1024 | bytes 1024 | tf_op jit(solution)/shard_map/project_peer/pallas_call | solution.py:110
  61.4 3.4 %collective-permute-start.5 = (bf16[256,256]{1,0:T(8,128)(2,1)S(1)}, bf16[256,256]{1,0:T(8,128)(2,1)S(1)}, u32[]{:S(2)}, u32[]{:S(2)}) collective-permute-start(bf16[256,256]{1,0:T(8,128)(2,1)S(1)} %get-tuple-element.60.refs_6_), channel_id=1, source_target_pairs={{0,4},{4,8},{8,12},{12,16},{16,20},{20,24},{24,28},{28,32},{32,36}... | collective-permute-start | bytes 393224 | tf_op jit(solution)/shard_map/ppermute | solution.py:263
  64.8 4.6 %collective-permute-start.6 = (bf16[256,256]{1,0:T(8,128)(2,1)S(1)}, bf16[256,256]{1,0:T(8,128)(2,1)S(1)}, u32[]{:S(2)}, u32[]{:S(2)}) collective-permute-start(bf16[256,256]{1,0:T(8,128)(2,1)S(1)} %get-tuple-element.60.refs_6_), channel_id=1, source_target_pairs={{0,8},{4,12},{8,16},{12,20},{16,24},{20,28},{24,32},{28,36},{32,40... | collective-permute-start | bytes 393224 | tf_op jit(solution)/shard_map/ppermute | solution.py:263
  69.5 0.6 transform_taps.1.refs_14_
  70.1 2.1 %collective-permute-done.2.peer = bf16[128,2048]{1,0:T(8,128)(2,1)S(1)} collective-permute-done((bf16[128,2048]{1,0:T(8,128)(2,1)S(1)}, bf16[128,2048]{1,0:T(8,128)(2,1)S(1)}, u32[]{:S(2)}, u32[]{:S(2)}) %collective-permute-start.2) | collective-permute-done | bytes 524320 | tf_op jit(solution)/shard_map/ppermute | solution.py:258
  72.2 1.1 collective-permute-done.5.refs_3_
  73.3 3.4 %collective-permute-done.6.refs_0_ = bf16[256,256]{1,0:T(8,128)(2,1)S(1)} collective-permute-done((bf16[256,256]{1,0:T(8,128)(2,1)S(1)}, bf16[256,256]{1,0:T(8,128)(2,1)S(1)}, u32[]{:S(2)}, u32[]{:S(2)}) %collective-permute-start.6) | collective-permute-done | bytes 131104 | tf_op jit(solution)/shard_map/ppermute | solution.py:263
  76.7 0.0 collective-permute-start.10
  76.7 0.0 collective-permute-done.8.peer_sibling
  76.7 4.3 %project_peer.5 = (bf16[256,256]{1,0:T(8,128)(2,1)S(1)}, bf16[256,256]{1,0:T(8,128)(2,1)S(1)}) custom-call(s32[4]{0:T(128)S(1)} %pad_add_fusion.order, bf16[256,2048]{1,0:T(8,128)(2,1)} %collective-permute-done.7.peer, bf16[256,2048]{1,0:T(8,128)(2,1)S(1)} %collective-permute-done.8.peer_sibling, f32[3,256,256]{2,1,0:T(8,128)S(1)} %get-tuple-element.50.known, ...), custom_call_target="tpu_custom_call" | custom-call | flops 1024 | bytes 1024 | tf_op jit(solution)/shard_map/project_peer/pallas_call | solution.py:110
  81.0 4.9 %collective-permute-done.11.peer = bf16[128,2048]{1,0:T(8,128)(2,1)S(1)} collective-permute-done((bf16[128,2048]{1,0:T(8,128)(2,1)S(1)}, bf16[128,2048]{1,0:T(8,128)(2,1)S(1)}, u32[]{:S(2)}, u32[]{:S(2)}) %collective-permute-start.11) | collective-permute-done | bytes 524320 | tf_op jit(solution)/shard_map/ppermute | solution.py:258
  85.9 0.0 collective-permute-start.12
  85.9 0.0 collective-permute-done.10.peer_sibling
  85.9 2.2 %project_peer.6 = (bf16[128,256]{1,0:T(8,128)(2,1)S(1)}, bf16[128,256]{1,0:T(8,128)(2,1)S(1)}) custom-call(s32[4]{0:T(128)S(1)} %pad_add_fusion.order, bf16[128,2048]{1,0:T(8,128)(2,1)S(1)} %collective-permute-done.2.peer, bf16[128,2048]{1,0:T(8,128)(2,1)S(1)} %collective-permute-done.10.peer_sibling, f32[3,128,256]{2,1,0:T(8,128)S(1)} %get-tuple-element.53.known, ...), custom_call_target="tpu_custom_call" | custom-call | flops 1024 | bytes 1024 | tf_op jit(solution)/shard_map/project_peer/pallas_call | solution.py:110
  88.1 1.9 %collective-permute-start.14 = (bf16[256,256]{1,0:T(8,128)(2,1)S(1)}, bf16[256,256]{1,0:T(8,128)(2,1)S(1)}, u32[]{:S(2)}, u32[]{:S(2)}) collective-permute-start(bf16[256,256]{1,0:T(8,128)(2,1)S(1)} %get-tuple-element.61.refs_7_), channel_id=1, source_target_pairs={{0,4},{4,8},{8,12},{12,16},{16,20},{20,24},{24,28},{28,32},{32,36}... | collective-permute-start | bytes 393224 | tf_op jit(solution)/shard_map/ppermute | solution.py:263
  90.1 1.9 %collective-permute-start.9 = (bf16[256,256]{1,0:T(8,128)(2,1)S(1)}, bf16[256,256]{1,0:T(8,128)(2,1)S(1)}, u32[]{:S(2)}, u32[]{:S(2)}) collective-permute-start(bf16[256,256]{1,0:T(8,128)(2,1)S(1)} %get-tuple-element.61.refs_7_), channel_id=1, source_target_pairs={{0,8},{4,12},{8,16},{12,20},{16,24},{20,28},{24,32},{28,36},{32,40... | collective-permute-start | bytes 393224 | tf_op jit(solution)/shard_map/ppermute | solution.py:263
  92.0 0.0 collective-permute-done.12.peer_sibling
  92.0 0.0 copy-start.4
  92.0 2.2 %project_peer.7 = (bf16[128,256]{1,0:T(8,128)(2,1)S(1)}, bf16[128,256]{1,0:T(8,128)(2,1)S(1)}) custom-call(s32[4]{0:T(128)S(1)} %pad_add_fusion.order, bf16[128,2048]{1,0:T(8,128)(2,1)S(1)} %collective-permute-done.11.peer, bf16[128,2048]{1,0:T(8,128)(2,1)S(1)} %collective-permute-done.12.peer_sibling, f32[3,128,256]{2,1,0:T(8,128)S(1)} %get-tuple-element.57.known, ...), custom_call_target="tpu_custom_call" | custom-call | flops 1024 | bytes 1024 | tf_op jit(solution)/shard_map/project_peer/pallas_call | solution.py:110
  94.3 7.1 %collective-permute-start.13 = (bf16[256,256]{1,0:T(8,128)(2,1)S(1)}, bf16[256,256]{1,0:T(8,128)(2,1)S(1)}, u32[]{:S(2)}, u32[]{:S(2)}) collective-permute-start(bf16[256,256]{1,0:T(8,128)(2,1)S(1)} %constant_dynamic-update-slice_fusion), channel_id=1, source_target_pairs={{0,8},{4,12},{8,16},{12,20},{16,24},{20,28},{24,32},{28,36},{32,40... | collective-permute-start | bytes 393224 | tf_op jit(solution)/shard_map/ppermute | solution.py:263
  101.4 2.5 %collective-permute-start.15 = (bf16[256,256]{1,0:T(8,128)(2,1)S(1)}, bf16[256,256]{1,0:T(8,128)(2,1)S(1)}, u32[]{:S(2)}, u32[]{:S(2)}) collective-permute-start(bf16[256,256]{1,0:T(8,128)(2,1)S(1)} %constant_dynamic-update-slice_fusion), channel_id=1, source_target_pairs={{0,4},{4,8},{8,12},{12,16},{16,20},{20,24},{24,28},{28,32},{32,36}... | collective-permute-start | bytes 393224 | tf_op jit(solution)/shard_map/ppermute | solution.py:263
  103.9 0.0 collective-permute-done.14.refs_4_
  103.9 3.0 %collective-permute-done.13.refs_2_ = bf16[256,256]{1,0:T(8,128)(2,1)S(1)} collective-permute-done((bf16[256,256]{1,0:T(8,128)(2,1)S(1)}, bf16[256,256]{1,0:T(8,128)(2,1)S(1)}, u32[]{:S(2)}, u32[]{:S(2)}) %collective-permute-start.13) | collective-permute-done | bytes 131104 | tf_op jit(solution)/shard_map/ppermute | solution.py:263
  106.9 6.3 %collective-permute-done.15.refs_5_ = bf16[256,256]{1,0:T(8,128)(2,1)S(1)} collective-permute-done((bf16[256,256]{1,0:T(8,128)(2,1)S(1)}, bf16[256,256]{1,0:T(8,128)(2,1)S(1)}, u32[]{:S(2)}, u32[]{:S(2)}) %collective-permute-start.15) | collective-permute-done | bytes 131104 | tf_op jit(solution)/shard_map/ppermute | solution.py:263
  113.2 3.9 %convolve.1 = bf16[768,256]{1,0:T(8,128)(2,1)} custom-call(bf16[256,256]{1,0:T(8,128)(2,1)S(1)} %collective-permute-done.6.refs_0_, bf16[256,256]{1,0:T(8,128)(2,1)S(1)} %collective-permute-done.9.refs_1_, bf16[256,256]{1,0:T(8,128)(2,1)S(1)} %collective-permute-done.13.refs_2_, bf16[256,256]{1,0:T(8,128)(2,1)S(1)} %collective-permute-done.5.refs_3_, ...), custom_call_target="tpu_custom_call" | custom-call | flops 1024 | bytes 1024 | tf_op jit(solution)/shard_map/convolve/pallas_call | solution.py:209
  (12 shorter events, 0.1 us)
Async XLA Ops:
  0.0 8.0 %collective-permute-start.4 = (bf16[768,2048]{1,0:T(8,128)(2,1)}, bf16[768,2048]{1,0:T(8,128)(2,1)}, u32[]{:S(2)}, u32[]{:S(2)}) collective-permute-start(bf16[768,2048]{1,0:T(8,128)(2,1)} %own.1), channel_id=1, source_target_pairs={{0,1},{1,0},{2,3},{3,2},{4,5},{5,4},{6,7},{7,6},{8,9},{9,8},{10,11... | collective-permute-start | bytes 9437192 | tf_op jit(solution)/shard_map/ppermute | solution.py:247
  0.0 5.5 %collective-permute-start = (bf16[48,256]{1,0:T(8,128)(2,1)}, bf16[48,256]{1,0:T(8,128)(2,1)S(1)}, u32[]{:S(2)}, u32[]{:S(2)}) collective-permute-start(bf16[48,256]{1,0:T(8,128)(2,1)} %param.7), channel_id=1, source_target_pairs={{0,16},{4,20},{8,24},{12,28},{16,0},{20,4},{24,8},{28,12},{32,48},... | collective-permute-start | bytes 73736 | tf_op jit(solution)/shard_map/ppermute | solution.py:224
  5.5 27.4 %copy-start.1 = (bf16[768,2048]{1,0:T(8,128)(2,1)S(1)}, bf16[768,2048]{1,0:T(8,128)(2,1)}, u32[]{:S(2)}) copy-start(bf16[768,2048]{1,0:T(8,128)(2,1)} %own.1) | copy-start | bytes 9437188
  6.5 26.4 %collective-permute-start.1 = (bf16[256,2048]{1,0:T(8,128)(2,1)}, bf16[256,2048]{1,0:T(8,128)(2,1)}, u32[]{:S(2)}, u32[]{:S(2)}) collective-permute-start(bf16[256,2048]{1,0:T(8,128)(2,1)} %slice.12), channel_id=1, source_target_pairs={{0,2},{1,3},{2,0},{3,1},{4,6},{5,7},{6,4},{7,5},{8,10},{9,11},{10,... | collective-permute-start | bytes 3145736 | tf_op jit(solution)/shard_map/ppermute | solution.py:258
  10.3 44.2 %collective-permute-start.7 = (bf16[256,2048]{1,0:T(8,128)(2,1)}, bf16[256,2048]{1,0:T(8,128)(2,1)}, u32[]{:S(2)}, u32[]{:S(2)}) collective-permute-start(bf16[256,2048]{1,0:T(8,128)(2,1)} %slice.14), channel_id=1, source_target_pairs={{0,2},{1,3},{2,0},{3,1},{4,6},{5,7},{6,4},{7,5},{8,10},{9,11},{10,... | collective-permute-start | bytes 3145736 | tf_op jit(solution)/shard_map/ppermute | solution.py:258
  32.8 24.0 %collective-permute-start.3 = (bf16[256,2048]{1,0:T(8,128)(2,1)}, bf16[256,2048]{1,0:T(8,128)(2,1)}, u32[]{:S(2)}, u32[]{:S(2)}) collective-permute-start(bf16[256,2048]{1,0:T(8,128)(2,1)} %collective-permute-done.1.peer), channel_id=1, source_target_pairs={{0,1},{1,0},{2,3},{3,2},{4,5},{5,4},{6,7},{7,6},{8,9},{9,8},{10,11... | collective-permute-start | bytes 3145736 | tf_op jit(solution)/shard_map/ppermute | solution.py:266
  32.9 4.6 %copy-start = (bf16[8192,3,256]{2,0,1:T(8,128)(2,1)S(1)}, bf16[8192,3,256]{2,0,1:T(8,128)(2,1)}, u32[]{:S(2)}) copy-start(bf16[8192,3,256]{2,0,1:T(8,128)(2,1)} %param.6) | copy-start | bytes 37748740
  54.6 22.2 %collective-permute-start.8 = (bf16[256,2048]{1,0:T(8,128)(2,1)}, bf16[256,2048]{1,0:T(8,128)(2,1)S(1)}, u32[]{:S(2)}, u32[]{:S(2)}) collective-permute-start(bf16[256,2048]{1,0:T(8,128)(2,1)} %collective-permute-done.7.peer), channel_id=1, source_target_pairs={{0,1},{1,0},{2,3},{3,2},{4,5},{5,4},{6,7},{7,6},{8,9},{9,8},{10,11... | collective-permute-start | bytes 3145736 | tf_op jit(solution)/shard_map/ppermute | solution.py:266
  54.6 17.6 %collective-permute-start.2 = (bf16[128,2048]{1,0:T(8,128)(2,1)S(1)}, bf16[128,2048]{1,0:T(8,128)(2,1)S(1)}, u32[]{:S(2)}, u32[]{:S(2)}) collective-permute-start(bf16[128,2048]{1,0:T(8,128)(2,1)S(1)} %slice.13), channel_id=1, source_target_pairs={{0,2},{1,3},{2,0},{3,1},{4,6},{5,7},{6,4},{7,5},{8,10},{9,11},{10,... | collective-permute-start | bytes 1572872 | tf_op jit(solution)/shard_map/ppermute | solution.py:258
  55.5 14.0 %copy-start.2 = (bf16[4,2,4,48,256]{4,3,2,1,0:T(8,128)(2,1)S(1)}, bf16[4,2,4,48,256]{4,3,2,1,0:T(8,128)(2,1)}, u32[]{:S(2)}) copy-start(bf16[4,2,4,48,256]{4,3,2,1,0:T(8,128)(2,1)} %copy.6) | copy-start | bytes 2359300
  55.5 14.0 %copy-start.3 = (bf16[512,256]{1,0:T(8,128)(2,1)S(1)}, bf16[512,256]{1,0:T(8,128)(2,1)}, u32[]{:S(2)}) copy-start(bf16[512,256]{1,0:T(8,128)(2,1)} %constant.23.clone.forward.refs_15_) | copy-start | bytes 786436
  55.5 30.4 %collective-permute-start.11 = (bf16[128,2048]{1,0:T(8,128)(2,1)S(1)}, bf16[128,2048]{1,0:T(8,128)(2,1)S(1)}, u32[]{:S(2)}, u32[]{:S(2)}) collective-permute-start(bf16[128,2048]{1,0:T(8,128)(2,1)S(1)} %slice.15), channel_id=1, source_target_pairs={{0,2},{1,3},{2,0},{3,1},{4,6},{5,7},{6,4},{7,5},{8,10},{9,11},{10,... | collective-permute-start | bytes 1572872 | tf_op jit(solution)/shard_map/ppermute | solution.py:258
  61.4 11.9 %collective-permute-start.5 = (bf16[256,256]{1,0:T(8,128)(2,1)S(1)}, bf16[256,256]{1,0:T(8,128)(2,1)S(1)}, u32[]{:S(2)}, u32[]{:S(2)}) collective-permute-start(bf16[256,256]{1,0:T(8,128)(2,1)S(1)} %get-tuple-element.60.refs_6_), channel_id=1, source_target_pairs={{0,4},{4,8},{8,12},{12,16},{16,20},{20,24},{24,28},{28,32},{32,36}... | collective-permute-start | bytes 393224 | tf_op jit(solution)/shard_map/ppermute | solution.py:263
  64.8 11.9 %collective-permute-start.6 = (bf16[256,256]{1,0:T(8,128)(2,1)S(1)}, bf16[256,256]{1,0:T(8,128)(2,1)S(1)}, u32[]{:S(2)}, u32[]{:S(2)}) collective-permute-start(bf16[256,256]{1,0:T(8,128)(2,1)S(1)} %get-tuple-element.60.refs_6_), channel_id=1, source_target_pairs={{0,8},{4,12},{8,16},{12,20},{16,24},{20,28},{24,32},{28,36},{32,40... | collective-permute-start | bytes 393224 | tf_op jit(solution)/shard_map/ppermute | solution.py:263
  76.7 9.2 %collective-permute-start.10 = (bf16[128,2048]{1,0:T(8,128)(2,1)S(1)}, bf16[128,2048]{1,0:T(8,128)(2,1)S(1)}, u32[]{:S(2)}, u32[]{:S(2)}) collective-permute-start(bf16[128,2048]{1,0:T(8,128)(2,1)S(1)} %collective-permute-done.2.peer), channel_id=1, source_target_pairs={{0,1},{1,0},{2,3},{3,2},{4,5},{5,4},{6,7},{7,6},{8,9},{9,8},{10,11... | collective-permute-start | bytes 1572872 | tf_op jit(solution)/shard_map/ppermute | solution.py:266
  85.9 6.1 %collective-permute-start.12 = (bf16[128,2048]{1,0:T(8,128)(2,1)S(1)}, bf16[128,2048]{1,0:T(8,128)(2,1)S(1)}, u32[]{:S(2)}, u32[]{:S(2)}) collective-permute-start(bf16[128,2048]{1,0:T(8,128)(2,1)S(1)} %collective-permute-done.11.peer), channel_id=1, source_target_pairs={{0,1},{1,0},{2,3},{3,2},{4,5},{5,4},{6,7},{7,6},{8,9},{9,8},{10,11... | collective-permute-start | bytes 1572872 | tf_op jit(solution)/shard_map/ppermute | solution.py:266
  88.1 15.7 %collective-permute-start.14 = (bf16[256,256]{1,0:T(8,128)(2,1)S(1)}, bf16[256,256]{1,0:T(8,128)(2,1)S(1)}, u32[]{:S(2)}, u32[]{:S(2)}) collective-permute-start(bf16[256,256]{1,0:T(8,128)(2,1)S(1)} %get-tuple-element.61.refs_7_), channel_id=1, source_target_pairs={{0,4},{4,8},{8,12},{12,16},{16,20},{20,24},{24,28},{28,32},{32,36}... | collective-permute-start | bytes 393224 | tf_op jit(solution)/shard_map/ppermute | solution.py:263
  90.1 13.8 %collective-permute-start.9 = (bf16[256,256]{1,0:T(8,128)(2,1)S(1)}, bf16[256,256]{1,0:T(8,128)(2,1)S(1)}, u32[]{:S(2)}, u32[]{:S(2)}) collective-permute-start(bf16[256,256]{1,0:T(8,128)(2,1)S(1)} %get-tuple-element.61.refs_7_), channel_id=1, source_target_pairs={{0,8},{4,12},{8,16},{12,20},{16,24},{20,28},{24,32},{28,36},{32,40... | collective-permute-start | bytes 393224 | tf_op jit(solution)/shard_map/ppermute | solution.py:263
  92.0 21.1 %copy-start.4 = (bf16[256,512]{1,0:T(8,128)(2,1)S(1)}, bf16[256,512]{1,0:T(8,128)(2,1)}, u32[]{:S(2)}) copy-start(bf16[256,512]{1,0:T(8,128)(2,1)} %constant.24.clone.refs_16_) | copy-start | bytes 786436
  94.3 12.6 %collective-permute-start.13 = (bf16[256,256]{1,0:T(8,128)(2,1)S(1)}, bf16[256,256]{1,0:T(8,128)(2,1)S(1)}, u32[]{:S(2)}, u32[]{:S(2)}) collective-permute-start(bf16[256,256]{1,0:T(8,128)(2,1)S(1)} %constant_dynamic-update-slice_fusion), channel_id=1, source_target_pairs={{0,8},{4,12},{8,16},{12,20},{16,24},{20,28},{24,32},{28,36},{32,40... | collective-permute-start | bytes 393224 | tf_op jit(solution)/shard_map/ppermute | solution.py:263
  101.4 11.8 %collective-permute-start.15 = (bf16[256,256]{1,0:T(8,128)(2,1)S(1)}, bf16[256,256]{1,0:T(8,128)(2,1)S(1)}, u32[]{:S(2)}, u32[]{:S(2)}) collective-permute-start(bf16[256,256]{1,0:T(8,128)(2,1)S(1)} %constant_dynamic-update-slice_fusion), channel_id=1, source_target_pairs={{0,4},{4,8},{8,12},{12,16},{16,20},{20,24},{24,28},{28,32},{32,36}... | collective-permute-start | bytes 393224 | tf_op jit(solution)/shard_map/ppermute | solution.py:263

commit v2 on v1

--- a/solution.py
+++ b/solution.py
@@ -12,7 +12,12 @@
 WHOLE = pl.BlockSpec(memory_space=pltpu.VMEM)
 SCALAR = pl.BlockSpec(memory_space=pltpu.SMEM)
 SMALL = pl.CostEstimate(flops=1024, bytes_accessed=1024, transcendentals=0)
-CHUNKS = ((0, 256), (256, 256), (512, 128), (640, 128))
+SIZES = (320, 384, 64)
+CHUNKS = tuple((sum(SIZES[:turn]), size) for turn, size in enumerate(SIZES))
+GROUPS = ((0, 1), (2,))
+BEFORE_SEND = ((), ("sibling",), ("arrived0",))
+BEFORE_PASS = (("taps",), ("product0", "spectrum"), ("product1",))
+BEFORE_START = ("both",)
 PEER = [(0, 2), (1, 3), (2, 0), (3, 1)]
 SIBLING = [(0, 1), (1, 0), (2, 3), (3, 2)]
 
@@ -160,16 +165,17 @@
         )
     half = BLOCK // 2
     rows = 8
-    for sign in (0, 1):
+    lanes = signal.shape[1]
+    for sign, lane in [(sign, lane) for sign in (0, 1) for lane in range(0, signal.shape[1], lanes)]:
 
         def mix(turn, carry):
             base = pl.multiple_of(sign * half + turn * rows, rows)
-            cos_at = pl.ds(base, rows)
-            sin_at = pl.ds(base + BLOCK, rows)
+            cos_at = pl.ds(base, rows), slice(lane, lane + lanes)
+            sin_at = pl.ds(base + BLOCK, rows), slice(lane, lane + lanes)
             pairs = []
             for pair in range(n_blocks - 1):
-                near_cos, near_sin = spectrum[pair, cos_at], spectrum[pair, sin_at]
-                far_cos, far_sin = spectrum[pair + 1, cos_at], spectrum[pair + 1, sin_at]
+                near_cos, near_sin = spectrum[pair, *cos_at], spectrum[pair, *sin_at]
+                far_cos, far_sin = spectrum[pair + 1, *cos_at], spectrum[pair + 1, *sin_at]
                 if sign == 0:
                     pairs.append((near_cos - far_sin, near_sin + far_cos))
                 else:
@@ -178,12 +184,12 @@
                 cos_sum = sin_sum = None
                 for i in range(n_taps):
                     c, s = pairs[n_taps - 1 + j - i]
-                    hc, hs = taps[i, cos_at], taps[i, sin_at]
+                    hc, hs = taps[i, *cos_at], taps[i, *sin_at]
                     cc, ss = c * hc - s * hs, c * hs + s * hc
                     cos_sum = cc if cos_sum is None else cos_sum + cc
                     sin_sum = ss if sin_sum is None else sin_sum + ss
-                mixed[j, cos_at] = cos_sum
-                mixed[j, sin_at] = sin_sum
+                mixed[j, *cos_at] = cos_sum
+                mixed[j, *sin_at] = sin_sum
             return carry
 
         lax.fori_loop(0, half // rows, mix, 0)
@@ -192,10 +198,10 @@
     ]
     at = 0
     for query in queries:
-        for row in range(0, query.shape[0], 128):
+        for row in range(0, query.shape[0], 32):
             block, offset = (at + row) // BLOCK, (at + row) % BLOCK
-            out[at + row : at + row + 128] = (
-                query[row : row + 128].astype(jnp.float32) * convolved[block][offset : offset + 128]
+            out[at + row : at + row + 32] = (
+                query[row : row + 32].astype(jnp.float32) * convolved[block][offset : offset + 32]
             ).astype(jnp.bfloat16)
         at += query.shape[0]
 
@@ -242,47 +248,41 @@
     weight = jnp.transpose(in_weight, (1, 0, 2))
     forward, inverse = spectral_tables()
 
-    together = lax.optimization_barrier
-    both = pair_taps(filter_taps)
-    sibling = lax.ppermute(features, "ch", SIBLING)
-    arrived = []
+    have = {"features": features}
+
+    def gate(name, needed):
+        names = [name] + [n for n in needed if n != name]
+        if len(names) > 1:
+            for n, value in zip(names, lax.optimization_barrier([have[n] for n in names])):
+                have[n] = value
+        return have[name]
+
+    have["both"] = pair_taps(filter_taps)
+    have["sibling"] = lax.ppermute(features, "ch", SIBLING)
     for turn, (at, rows) in enumerate(CHUNKS):
-        whole = features
-        if turn == 1:
-            whole, sibling = together((features, sibling))
-        elif turn >= 2:
-            whole, arrived[turn - 2] = together((features, arrived[turn - 2]))
-        piece = whole[at : at + rows]
-        if turn == 0:
-            piece, both = together((piece, both))
-        arrived.append(lax.ppermute(piece, "ch", PEER))
-    taps = exchange_taps(both)
-    known = list(project_own(order, features, sibling, weight))
-
-    def send(group):
-        return [lax.ppermute(group, "ctx", ahead[by]) for by in (0, 1)]
-
-    def finish(turn, peer):
+        have["piece"] = gate("features", BEFORE_SEND[turn])[at : at + rows]
+        have[f"arrived{turn}"] = lax.ppermute(gate("piece", BEFORE_START if turn == 0 else ()), "ch", PEER)
+
+    have["taps"] = exchange_taps(have["both"])
+    have["spectrum"] = transform_taps(have["taps"], forward)
+    for turn, part in enumerate(project_own(order, have["features"], have["sibling"], weight)):
+        have[f"known{turn}"] = part
+    for turn in range(len(CHUNKS)):
+        peer = gate(f"arrived{turn}", BEFORE_PASS[turn])
         peer_sibling = lax.ppermute(peer, "ch", SIBLING)
-        return project_peer(order, peer, peer_sibling, known[turn], weight)
-
-    peer, taps = together((arrived[0], taps))
-    query_0, product_0 = finish(0, peer)
-    halo_0 = send(product_0)
-    peer, known[0], known[1] = together((arrived[1], known[0], known[1]))
-    query_1, product_1 = finish(1, peer)
-    spectrum = transform_taps(taps, forward)
-    peer, product_0, halo_0[0], halo_0[1], spectrum = together(
-        (arrived[2], product_0, halo_0[0], halo_0[1], spectrum)
-    )
-    query_2, product_2 = finish(2, peer)
-    halo_1 = send(product_1)
-    peer, product_1 = together((arrived[3], product_1))
-    query_3, product_3 = finish(3, peer)
-    halo_2 = send(jnp.concatenate([product_2, product_3], 0))
-    sources = [halo_0[1], halo_1[1], halo_2[1], halo_0[0], halo_1[0], halo_2[0]]
-    sources += [product_0, product_1, product_2, product_3]
-    return convolve(sources, [query_0, query_1, query_2, query_3], spectrum, forward, inverse)
+        known = have[f"known{turn}"]
+        query, product = project_peer(order, peer, peer_sibling, known, weight)
+        have[f"query{turn}"], have[f"product{turn}"] = query, product
+        for number, group in enumerate(GROUPS):
+            if group[-1] == turn:
+                parts = [have[f"product{member}"] for member in group]
+                together = jnp.concatenate(parts, 0) if len(parts) > 1 else parts[0]
+                have[f"near{number}"] = lax.ppermute(together, "ctx", ahead[0])
+                have[f"far{number}"] = lax.ppermute(together, "ctx", ahead[1])
+    sources = [have[f"{side}{number}"] for side in ("far", "near") for number in range(len(GROUPS))]
+    sources += [have[f"product{turn}"] for turn in range(len(CHUNKS))]
+    queries = [have[f"query{turn}"] for turn in range(len(CHUNKS))]
+    return convolve(sources, queries, have["spectrum"], forward, inverse)
 
 
 def solution(mesh):

time: 118 us -> 110 us (0.932)
  blocking collectives: 18.8 us -> 0 us
  waiting for transfers between devices: 31.6 us -> 40.7 us
  local copies, waits for them, and re-layouts: 10.4 us -> 12.9 us
    all_to_all x1 -> x0, blocking collectives: 18.8 us -> none  [exchange_taps(): lax.all_to_all(copies, 'ctx', 0, 0, axis_index_groups=groups, tiled=True)]
    all_to_all x0 -> x1, waiting for transfers between devices: none -> 9.21 us  [exchange_taps(): lax.all_to_all(copies, 'ctx', 0, 0, axis_index_groups=groups, tiled=True)]
    all_to_all x0 -> x1, starting transfers between devices: none -> 7.44 us  [exchange_taps(): lax.all_to_all(copies, 'ctx', 0, 0, axis_index_groups=groups, tiled=True)]
    ppermute x15 -> x11, starting transfers between devices: 25.8 us -> 19.2 us  [the longest x2 9.56 us: body(): have[f'far{number}'] = lax.ppermute(together, 'ctx', ahead[1])]
    unnamed x11 -> x13, local copies, waits for them, and re-layouts: 4.61 us -> 5.73 us
    slice x4 -> x3, local copies, waits for them, and re-layouts: 4.7 us -> 4.11 us  [body(): have['piece'] = gate('features', BEFORE_SEND[turn])[at:at + rows]]
    pallas_call x4 -> x3, Pallas kernels: 13.3 us -> 12.7 us  [project_peer(): pl.pallas_call(project_peer_kernel, out_shape=[jax.ShapeDtypeStruct((rows...]
    ppermute x15 -> x11, waiting for transfers between devices: 31.6 us -> 31.5 us  [the longest x3 21.3 us: body(): lax.ppermute(gate('piece', BEFORE_START if turn == 0 else ()), 'ch', PEER)]
  transfers between devices with their start and end apart: 16 -> 13, of which waited for: 8 -> 6; matrix products, arithmetic and copies ran while one was open for 6% -> 7% of each run, Pallas kernels for 19% -> 20%
where the time goes in v2:
time: 110 us
  waiting for transfers between devices  40.7 us (37%)
  starting transfers between devices  29.9 us (27%)
  Pallas kernels  26.1 us (24%)
  local copies, waits for them, and re-layouts  12.9 us (12%)
    ppermute x3, waiting for transfers between devices, body(): lax.ppermute(gate('piece', BEFORE_START if turn == 0 else ()), 'ch', PEER)  21.3 us
    pallas_call x3, Pallas kernels, project_peer(): pl.pallas_call(project_peer_kernel, out_shape=[jax.ShapeDtypeStruct((rows...  12.7 us
    ppermute x2, starting transfers between devices, body(): have[f'far{number}'] = lax.ppermute(together, 'ctx', ahead[1])  9.56 us
    all_to_all x1, waiting for transfers between devices, exchange_taps(): lax.all_to_all(copies, 'ctx', 0, 0, axis_index_groups=groups, tiled=True)  9.21 us
    pallas_call x1, Pallas kernels, project_own(): pl.pallas_call(project_own_kernel, out_shape=[jax.ShapeDtypeStruct((3, si...  8.92 us
    all_to_all x1, starting transfers between devices, exchange_taps(): lax.all_to_all(copies, 'ctx', 0, 0, axis_index_groups=groups, tiled=True)  7.44 us
    ppermute x2, starting transfers between devices, body(): have[f'near{number}'] = lax.ppermute(together, 'ctx', ahead[0])  6.54 us
    ppermute x2, waiting for transfers between devices, body(): have[f'near{number}'] = lax.ppermute(together, 'ctx', ahead[0])  5.95 us
  transfers between devices with their start and end apart: 13, of which 6 were waited for; matrix products, arithmetic and copies ran while one was open for 7% of the time, Pallas kernels for 20%

profile of v2, /device:TPU:64, one launch (start us, length us, event | category | flops | bytes accessed | tf_op | source)
XLA Modules:
  0.0 109.9 jit_solution(13437377312642053664)
XLA Ops:
  0.0 0.0 copy-start.5
  0.0 0.0 collective-permute-start
  0.0 3.3 %collective-permute-start.2 = (bf16[48,256]{1,0:T(8,128)(2,1)}, bf16[48,256]{1,0:T(8,128)(2,1)S(1)}, u32[]{:S(2)}, u32[]{:S(2)}) collective-permute-start(bf16[48,256]{1,0:T(8,128)(2,1)} %param.7), channel_id=1, source_target_pairs={{0,16},{4,20},{8,24},{12,28},{16,0},{20,4},{24,8},{28,12},{32,48},... | collective-permute-start | bytes 73736 | tf_op jit(solution)/shard_map/ppermute | solution.py:230
  3.3 0.0 copy-start.1
  3.3 2.7 %slice.10 = bf16[320,2048]{1,0:T(8,128)(2,1)} slice(bf16[768,2048]{1,0:T(8,128)(2,1)} %own), slice={[0:320], [0:2048]} | slice | bytes 2621440 | tf_op jit(solution)/shard_map/slice | solution.py:263
  6.0 0.0 collective-permute-done.2
  6.0 0.0 copy-done.5
  6.0 1.2 %collective-permute-start.3 = (bf16[320,2048]{1,0:T(8,128)(2,1)}, bf16[320,2048]{1,0:T(8,128)(2,1)}, u32[]{:S(2)}, u32[]{:S(2)}) collective-permute-start(bf16[320,2048]{1,0:T(8,128)(2,1)} %slice.10), channel_id=1, source_target_pairs={{0,2},{1,3},{2,0},{3,1},{4,6},{5,7},{6,4},{7,5},{8,10},{9,11},{10,... | collective-permute-start | bytes 3932168 | tf_op jit(solution)/shard_map/ppermute | solution.py:264
  7.3 0.9 broadcast_in_dim.2
  8.2 7.4 %all-to-all-start = ((bf16[16,2,48,256]{3,2,1,0:T(8,128)(2,1)}), bf16[16,2,48,256]{3,2,1,0:T(8,128)(2,1)}, u32[]{:S(2)}, u32[]{:S(2)}) async-start(bf16[16,2,48,256]{3,2,1,0:T(8,128)(2,1)} %broadcast_in_dim.2), calls=%async_computation | async-start | bytes 1572864 | tf_op jit(solution)/shard_map/all_to_all | solution.py:239
  15.7 0.0 collective-permute-done.sibling
  15.7 0.0 copy-done.1
  15.7 1.3 %slice.9 = bf16[384,2048]{1,0:T(8,128)(2,1)} slice(bf16[768,2048]{1,0:T(8,128)(2,1)S(1)} %copy-done.1), slice={[320:704], [0:2048]} | slice | bytes 3145728 | tf_op jit(solution)/shard_map/slice | solution.py:263
  17.0 0.0 copy-start.3
  17.0 0.9 collective-permute-start.1
  17.9 9.2 %all-to-all-done = bf16[16,2,48,256]{3,2,1,0:T(8,128)(2,1)} async-done(((bf16[16,2,48,256]{3,2,1,0:T(8,128)(2,1)}), bf16[16,2,48,256]{3,2,1,0:T(8,128)(2,1)}, u32[]{:S(2)}, u32[]{:S(2)}) %all-to-all-start) | async-done | bytes 786464 | tf_op jit(solution)/shard_map/all_to_all | solution.py:239
  27.1 2.1 %copy.6 = bf16[4,2,4,48,256]{4,3,2,1,0:T(8,128)(2,1)} copy(bf16[4,2,4,48,256]{4,3,1,2,0:T(8,128)(2,1)} %bitcast.7) | data formatting | bytes 1572864 | tf_op jit(solution)/shard_map/transpose | solution.py:240
  29.2 8.9 %collective-permute-done.3.peer = bf16[320,2048]{1,0:T(8,128)(2,1)} collective-permute-done((bf16[320,2048]{1,0:T(8,128)(2,1)}, bf16[320,2048]{1,0:T(8,128)(2,1)}, u32[]{:S(2)}, u32[]{:S(2)}) %collective-permute-start.3) | collective-permute-done | bytes 1310752 | tf_op jit(solution)/shard_map/ppermute | solution.py:264
  38.1 0.0 collective-permute-start.4
  38.1 0.1 pad_add_fusion.order
  38.1 0.0 copy-done.3
  38.1 0.0 copy-start.2
  38.1 1.1 %copy-done.2 = bf16[4,2,4,48,256]{4,3,2,1,0:T(8,128)(2,1)S(1)} copy-done((bf16[4,2,4,48,256]{4,3,2,1,0:T(8,128)(2,1)S(1)}, bf16[4,2,4,48,256]{4,3,2,1,0:T(8,128)(2,1)}, u32[]{:S(2)}) %copy-start.2) | copy-done | bytes 786456
  39.3 0.6 transform_taps.1.refs_10_
  39.9 0.0 copy-start
  39.9 4.6 %copy-done = bf16[8192,3,256]{2,0,1:T(8,128)(2,1)S(1)} copy-done((bf16[8192,3,256]{2,0,1:T(8,128)(2,1)S(1)}, bf16[8192,3,256]{2,0,1:T(8,128)(2,1)}, u32[]{:S(2)}) %copy-start) | copy-done | bytes 12582936
  44.4 8.9 %project_own.1 = (f32[3,320,256]{2,1,0:T(8,128)S(1)}, f32[3,384,256]{2,1,0:T(8,128)S(1)}, f32[3,64,256]{2,1,0:T(8,128)S(1)}) custom-call(s32[4]{0:T(128)S(1)} %pad_add_fusion.order, bf16[768,2048]{1,0:T(8,128)(2,1)S(1)} %copy-done.1, bf16[768,2048]{1,0:T(8,128)(2,1)} %collective-permute-done.sibling, bf16[3,8192,256]{2,1,0:T(8,128)(2,1)S(1)} %bitcast.11, ...), custom_call_target="tpu_custom_call" | custom-call | flops 1024 | bytes 1024 | tf_op jit(solution)/shard_map/project_own/pallas_call | solution.py:71
  53.4 0.0 collective-permute-done.4.peer_sibling
  53.4 5.2 %project_peer.3 = (bf16[320,256]{1,0:T(8,128)(2,1)S(1)}, bf16[320,256]{1,0:T(8,128)(2,1)S(1)}) custom-call(s32[4]{0:T(128)S(1)} %pad_add_fusion.order, bf16[320,2048]{1,0:T(8,128)(2,1)} %collective-permute-done.3.peer, bf16[320,2048]{1,0:T(8,128)(2,1)} %collective-permute-done.4.peer_sibling, f32[3,320,256]{2,1,0:T(8,128)S(1)} %get-tuple-element.33.known, ...), custom_call_target="tpu_custom_call" | custom-call | flops 1024 | bytes 1024 | tf_op jit(solution)/shard_map/project_peer/pallas_call | solution.py:115
  58.5 12.5 %collective-permute-done.1.peer = bf16[384,2048]{1,0:T(8,128)(2,1)} collective-permute-done((bf16[384,2048]{1,0:T(8,128)(2,1)}, bf16[384,2048]{1,0:T(8,128)(2,1)}, u32[]{:S(2)}, u32[]{:S(2)}) %collective-permute-start.1) | collective-permute-done | bytes 1572896 | tf_op jit(solution)/shard_map/ppermute | solution.py:264
  71.0 0.0 collective-permute-start.5
  71.0 0.9 collective-permute-start.7
  72.0 2.6 %collective-permute-done.5.peer_sibling = bf16[384,2048]{1,0:T(8,128)(2,1)S(1)} collective-permute-done((bf16[384,2048]{1,0:T(8,128)(2,1)}, bf16[384,2048]{1,0:T(8,128)(2,1)S(1)}, u32[]{:S(2)}, u32[]{:S(2)}) %collective-permute-start.5) | collective-permute-done | bytes 1572896 | tf_op jit(solution)/shard_map/ppermute | solution.py:272
  74.6 5.3 %project_peer.4 = (bf16[384,256]{1,0:T(8,128)(2,1)S(1)}, bf16[384,256]{1,0:T(8,128)(2,1)S(1)}) custom-call(s32[4]{0:T(128)S(1)} %pad_add_fusion.order, bf16[384,2048]{1,0:T(8,128)(2,1)} %collective-permute-done.1.peer, bf16[384,2048]{1,0:T(8,128)(2,1)S(1)} %collective-permute-done.5.peer_sibling, f32[3,384,256]{2,1,0:T(8,128)S(1)} %get-tuple-element.37.known, ...), custom_call_target="tpu_custom_call" | custom-call | flops 1024 | bytes 1024 | tf_op jit(solution)/shard_map/project_peer/pallas_call | solution.py:115
  79.9 3.4 %collective-permute-start.10 = (bf16[704,256]{1,0:T(8,128)(2,1)S(1)}, bf16[704,256]{1,0:T(8,128)(2,1)S(1)}, u32[]{:S(2)}, u32[]{:S(2)}) collective-permute-start(bf16[704,256]{1,0:T(8,128)(2,1)S(1)} %constant_dynamic-update-slice_fusion), channel_id=1, source_target_pairs={{0,4},{4,8},{8,12},{12,16},{16,20},{20,24},{24,28},{28,32},{32,36}... | collective-permute-start | bytes 1081352 | tf_op jit(solution)/shard_map/ppermute | solution.py:280
  83.3 4.6 %collective-permute-start.6 = (bf16[704,256]{1,0:T(8,128)(2,1)S(1)}, bf16[704,256]{1,0:T(8,128)(2,1)S(1)}, u32[]{:S(2)}, u32[]{:S(2)}) collective-permute-start(bf16[704,256]{1,0:T(8,128)(2,1)S(1)} %constant_dynamic-update-slice_fusion), channel_id=1, source_target_pairs={{0,8},{4,12},{8,16},{12,20},{16,24},{20,28},{24,32},{28,36},{32,40... | collective-permute-start | bytes 1081352 | tf_op jit(solution)/shard_map/ppermute | solution.py:281
  88.0 0.0 collective-permute-done.7.peer
  88.0 0.1 collective-permute-start.8
  88.1 1.5 %collective-permute-done.8.peer_sibling = bf16[64,2048]{1,0:T(8,128)(2,1)S(1)} collective-permute-done((bf16[64,2048]{1,0:T(8,128)(2,1)S(1)}, bf16[64,2048]{1,0:T(8,128)(2,1)S(1)}, u32[]{:S(2)}, u32[]{:S(2)}) %collective-permute-start.8) | collective-permute-done | bytes 262176 | tf_op jit(solution)/shard_map/ppermute | solution.py:272
  89.6 2.3 %project_peer.5 = (bf16[64,256]{1,0:T(8,128)(2,1)S(1)}, bf16[64,256]{1,0:T(8,128)(2,1)S(1)}) custom-call(s32[4]{0:T(128)S(1)} %pad_add_fusion.order, bf16[64,2048]{1,0:T(8,128)(2,1)S(1)} %collective-permute-done.7.peer, bf16[64,2048]{1,0:T(8,128)(2,1)S(1)} %collective-permute-done.8.peer_sibling, f32[3,64,256]{2,1,0:T(8,128)S(1)} %get-tuple-element.40.known, ...), custom_call_target="tpu_custom_call" | custom-call | flops 1024 | bytes 1024 | tf_op jit(solution)/shard_map/project_peer/pallas_call | solution.py:115
  91.9 3.1 %collective-permute-start.11 = (bf16[64,256]{1,0:T(8,128)(2,1)S(1)}, bf16[64,256]{1,0:T(8,128)(2,1)S(1)}, u32[]{:S(2)}, u32[]{:S(2)}) collective-permute-start(bf16[64,256]{1,0:T(8,128)(2,1)S(1)} %get-tuple-element.41.refs_6_), channel_id=1, source_target_pairs={{0,4},{4,8},{8,12},{12,16},{16,20},{20,24},{24,28},{28,32},{32,36}... | collective-permute-start | bytes 98312 | tf_op jit(solution)/shard_map/ppermute | solution.py:280
  95.0 4.9 %collective-permute-start.9 = (bf16[64,256]{1,0:T(8,128)(2,1)S(1)}, bf16[64,256]{1,0:T(8,128)(2,1)S(1)}, u32[]{:S(2)}, u32[]{:S(2)}) collective-permute-start(bf16[64,256]{1,0:T(8,128)(2,1)S(1)} %get-tuple-element.41.refs_6_), channel_id=1, source_target_pairs={{0,8},{4,12},{8,16},{12,20},{16,24},{20,28},{24,32},{28,36},{32,40... | collective-permute-start | bytes 98312 | tf_op jit(solution)/shard_map/ppermute | solution.py:281
  100.0 5.9 %collective-permute-done.11.refs_3_ = bf16[64,256]{1,0:T(8,128)(2,1)S(1)} collective-permute-done((bf16[64,256]{1,0:T(8,128)(2,1)S(1)}, bf16[64,256]{1,0:T(8,128)(2,1)S(1)}, u32[]{:S(2)}, u32[]{:S(2)}) %collective-permute-start.11) | collective-permute-done | bytes 32800 | tf_op jit(solution)/shard_map/ppermute | solution.py:280
  105.9 0.0 collective-permute-done.9.refs_1_
  105.9 0.0 collective-permute-done.10.refs_2_
  105.9 0.0 collective-permute-done.6.refs_0_
  105.9 0.0 copy-done.4
  105.9 3.9 %convolve.1 = bf16[768,256]{1,0:T(8,128)(2,1)} custom-call(bf16[704,256]{1,0:T(8,128)(2,1)S(1)} %collective-permute-done.6.refs_0_, bf16[64,256]{1,0:T(8,128)(2,1)S(1)} %collective-permute-done.9.refs_1_, bf16[704,256]{1,0:T(8,128)(2,1)S(1)} %collective-permute-done.10.refs_2_, bf16[64,256]{1,0:T(8,128)(2,1)S(1)} %collective-permute-done.11.refs_3_, ...), custom_call_target="tpu_custom_call" | custom-call | flops 1024 | bytes 1024 | tf_op jit(solution)/shard_map/convolve/pallas_call | solution.py:215
  (5 shorter events, 0.1 us)
Async XLA Ops:
  0.0 6.0 %copy-start.5 = (bf16[48,256]{1,0:T(8,128)(2,1)S(1)}, bf16[48,256]{1,0:T(8,128)(2,1)}, u32[]{:S(2)}) copy-start(bf16[48,256]{1,0:T(8,128)(2,1)} %param.7) | copy-start | bytes 73732
  0.0 15.7 %collective-permute-start = (bf16[768,2048]{1,0:T(8,128)(2,1)}, bf16[768,2048]{1,0:T(8,128)(2,1)}, u32[]{:S(2)}, u32[]{:S(2)}) collective-permute-start(bf16[768,2048]{1,0:T(8,128)(2,1)} %own), channel_id=1, source_target_pairs={{0,1},{1,0},{2,3},{3,2},{4,5},{5,4},{6,7},{7,6},{8,9},{9,8},{10,11... | collective-permute-start | bytes 9437192 | tf_op jit(solution)/shard_map/ppermute | solution.py:261
  0.0 6.0 %collective-permute-start.2 = (bf16[48,256]{1,0:T(8,128)(2,1)}, bf16[48,256]{1,0:T(8,128)(2,1)S(1)}, u32[]{:S(2)}, u32[]{:S(2)}) collective-permute-start(bf16[48,256]{1,0:T(8,128)(2,1)} %param.7), channel_id=1, source_target_pairs={{0,16},{4,20},{8,24},{12,28},{16,0},{20,4},{24,8},{28,12},{32,48},... | collective-permute-start | bytes 73736 | tf_op jit(solution)/shard_map/ppermute | solution.py:230
  3.3 12.4 %copy-start.1 = (bf16[768,2048]{1,0:T(8,128)(2,1)S(1)}, bf16[768,2048]{1,0:T(8,128)(2,1)}, u32[]{:S(2)}) copy-start(bf16[768,2048]{1,0:T(8,128)(2,1)} %own) | copy-start | bytes 9437188
  6.0 32.0 %collective-permute-start.3 = (bf16[320,2048]{1,0:T(8,128)(2,1)}, bf16[320,2048]{1,0:T(8,128)(2,1)}, u32[]{:S(2)}, u32[]{:S(2)}) collective-permute-start(bf16[320,2048]{1,0:T(8,128)(2,1)} %slice.10), channel_id=1, source_target_pairs={{0,2},{1,3},{2,0},{3,1},{4,6},{5,7},{6,4},{7,5},{8,10},{9,11},{10,... | collective-permute-start | bytes 3932168 | tf_op jit(solution)/shard_map/ppermute | solution.py:264
  8.2 18.9 %all-to-all-start = ((bf16[16,2,48,256]{3,2,1,0:T(8,128)(2,1)}), bf16[16,2,48,256]{3,2,1,0:T(8,128)(2,1)}, u32[]{:S(2)}, u32[]{:S(2)}) async-start(bf16[16,2,48,256]{3,2,1,0:T(8,128)(2,1)} %broadcast_in_dim.2), calls=%async_computation | async-start | bytes 1572864 | tf_op jit(solution)/shard_map/all_to_all | solution.py:239
  17.0 21.1 %copy-start.3 = (bf16[512,256]{1,0:T(8,128)(2,1)S(1)}, bf16[512,256]{1,0:T(8,128)(2,1)}, u32[]{:S(2)}) copy-start(bf16[512,256]{1,0:T(8,128)(2,1)} %constant.23.clone.forward.refs_11_) | copy-start | bytes 786436
  17.0 54.0 %collective-permute-start.1 = (bf16[384,2048]{1,0:T(8,128)(2,1)}, bf16[384,2048]{1,0:T(8,128)(2,1)}, u32[]{:S(2)}, u32[]{:S(2)}) collective-permute-start(bf16[384,2048]{1,0:T(8,128)(2,1)} %slice.9), channel_id=1, source_target_pairs={{0,2},{1,3},{2,0},{3,1},{4,6},{5,7},{6,4},{7,5},{8,10},{9,11},{10,... | collective-permute-start | bytes 4718600 | tf_op jit(solution)/shard_map/ppermute | solution.py:264
  38.1 15.3 %collective-permute-start.4 = (bf16[320,2048]{1,0:T(8,128)(2,1)}, bf16[320,2048]{1,0:T(8,128)(2,1)}, u32[]{:S(2)}, u32[]{:S(2)}) collective-permute-start(bf16[320,2048]{1,0:T(8,128)(2,1)} %collective-permute-done.3.peer), channel_id=1, source_target_pairs={{0,1},{1,0},{2,3},{3,2},{4,5},{5,4},{6,7},{7,6},{8,9},{9,8},{10,11... | collective-permute-start | bytes 3932168 | tf_op jit(solution)/shard_map/ppermute | solution.py:272
  38.1 1.1 %copy-start.2 = (bf16[4,2,4,48,256]{4,3,2,1,0:T(8,128)(2,1)S(1)}, bf16[4,2,4,48,256]{4,3,2,1,0:T(8,128)(2,1)}, u32[]{:S(2)}) copy-start(bf16[4,2,4,48,256]{4,3,2,1,0:T(8,128)(2,1)} %copy.6) | copy-start | bytes 2359300
  39.9 4.6 %copy-start = (bf16[8192,3,256]{2,0,1:T(8,128)(2,1)S(1)}, bf16[8192,3,256]{2,0,1:T(8,128)(2,1)}, u32[]{:S(2)}) copy-start(bf16[8192,3,256]{2,0,1:T(8,128)(2,1)} %param.6) | copy-start | bytes 37748740
  71.0 3.6 %collective-permute-start.5 = (bf16[384,2048]{1,0:T(8,128)(2,1)}, bf16[384,2048]{1,0:T(8,128)(2,1)S(1)}, u32[]{:S(2)}, u32[]{:S(2)}) collective-permute-start(bf16[384,2048]{1,0:T(8,128)(2,1)} %collective-permute-done.1.peer), channel_id=1, source_target_pairs={{0,1},{1,0},{2,3},{3,2},{4,5},{5,4},{6,7},{7,6},{8,9},{9,8},{10,11... | collective-permute-start | bytes 4718600 | tf_op jit(solution)/shard_map/ppermute | solution.py:272
  71.0 17.0 %collective-permute-start.7 = (bf16[64,2048]{1,0:T(8,128)(2,1)S(1)}, bf16[64,2048]{1,0:T(8,128)(2,1)S(1)}, u32[]{:S(2)}, u32[]{:S(2)}) collective-permute-start(bf16[64,2048]{1,0:T(8,128)(2,1)S(1)} %slice.11), channel_id=1, source_target_pairs={{0,2},{1,3},{2,0},{3,1},{4,6},{5,7},{6,4},{7,5},{8,10},{9,11},{10,... | collective-permute-start | bytes 786440 | tf_op jit(solution)/shard_map/ppermute | solution.py:264
  79.9 26.0 %collective-permute-start.10 = (bf16[704,256]{1,0:T(8,128)(2,1)S(1)}, bf16[704,256]{1,0:T(8,128)(2,1)S(1)}, u32[]{:S(2)}, u32[]{:S(2)}) collective-permute-start(bf16[704,256]{1,0:T(8,128)(2,1)S(1)} %constant_dynamic-update-slice_fusion), channel_id=1, source_target_pairs={{0,4},{4,8},{8,12},{12,16},{16,20},{20,24},{24,28},{28,32},{32,36}... | collective-permute-start | bytes 1081352 | tf_op jit(solution)/shard_map/ppermute | solution.py:280
  83.3 22.6 %collective-permute-start.6 = (bf16[704,256]{1,0:T(8,128)(2,1)S(1)}, bf16[704,256]{1,0:T(8,128)(2,1)S(1)}, u32[]{:S(2)}, u32[]{:S(2)}) collective-permute-start(bf16[704,256]{1,0:T(8,128)(2,1)S(1)} %constant_dynamic-update-slice_fusion), channel_id=1, source_target_pairs={{0,8},{4,12},{8,16},{12,20},{16,24},{20,28},{24,32},{28,36},{32,40... | collective-permute-start | bytes 1081352 | tf_op jit(solution)/shard_map/ppermute | solution.py:281
  88.0 1.6 %collective-permute-start.8 = (bf16[64,2048]{1,0:T(8,128)(2,1)S(1)}, bf16[64,2048]{1,0:T(8,128)(2,1)S(1)}, u32[]{:S(2)}, u32[]{:S(2)}) collective-permute-start(bf16[64,2048]{1,0:T(8,128)(2,1)S(1)} %collective-permute-done.7.peer), channel_id=1, source_target_pairs={{0,1},{1,0},{2,3},{3,2},{4,5},{5,4},{6,7},{7,6},{8,9},{9,8},{10,11... | collective-permute-start | bytes 786440 | tf_op jit(solution)/shard_map/ppermute | solution.py:272
  89.6 16.3 %copy-start.4 = (bf16[256,512]{1,0:T(8,128)(2,1)S(1)}, bf16[256,512]{1,0:T(8,128)(2,1)}, u32[]{:S(2)}) copy-start(bf16[256,512]{1,0:T(8,128)(2,1)} %constant.24.clone.refs_12_) | copy-start | bytes 786436
  91.9 14.0 %collective-permute-start.11 = (bf16[64,256]{1,0:T(8,128)(2,1)S(1)}, bf16[64,256]{1,0:T(8,128)(2,1)S(1)}, u32[]{:S(2)}, u32[]{:S(2)}) collective-permute-start(bf16[64,256]{1,0:T(8,128)(2,1)S(1)} %get-tuple-element.41.refs_6_), channel_id=1, source_target_pairs={{0,4},{4,8},{8,12},{12,16},{16,20},{20,24},{24,28},{28,32},{32,36}... | collective-permute-start | bytes 98312 | tf_op jit(solution)/shard_map/ppermute | solution.py:280
  95.0 10.9 %collective-permute-start.9 = (bf16[64,256]{1,0:T(8,128)(2,1)S(1)}, bf16[64,256]{1,0:T(8,128)(2,1)S(1)}, u32[]{:S(2)}, u32[]{:S(2)}) collective-permute-start(bf16[64,256]{1,0:T(8,128)(2,1)S(1)} %get-tuple-element.41.refs_6_), channel_id=1, source_target_pairs={{0,8},{4,12},{8,16},{12,20},{16,24},{20,28},{24,32},{28,36},{32,40... | collective-permute-start | bytes 98312 | tf_op jit(solution)/shard_map/ppermute | solution.py:281

commit v3 on v2

--- a/solution.py
+++ b/solution.py
@@ -9,6 +9,8 @@
 from jax.sharding import PartitionSpec as P
 
 BLOCK = 256
+ROWS = 8
+UNROLL = 16
 WHOLE = pl.BlockSpec(memory_space=pltpu.VMEM)
 SCALAR = pl.BlockSpec(memory_space=pltpu.SMEM)
 SMALL = pl.CostEstimate(flops=1024, bytes_accessed=1024, transcendentals=0)
@@ -164,7 +166,7 @@
             forward[...], signal[block * BLOCK : (block + 1) * BLOCK], preferred_element_type=jnp.float32
         )
     half = BLOCK // 2
-    rows = 8
+    rows = ROWS
     lanes = signal.shape[1]
     for sign, lane in [(sign, lane) for sign in (0, 1) for lane in range(0, signal.shape[1], lanes)]:
 
@@ -192,7 +194,7 @@
                 mixed[j, *sin_at] = sin_sum
             return carry
 
-        lax.fori_loop(0, half // rows, mix, 0)
+        lax.fori_loop(0, half // rows, mix, 0, unroll=UNROLL)
     convolved = [
         jnp.dot(inverse[...], mixed[j].astype(jnp.bfloat16), preferred_element_type=jnp.float32) for j in range(n_out)
     ]

time: 110 us -> 110 us (level)
  no operation moved by 1% of the time
where the time goes in v3:
time: 110 us; the launch traced here: 109 us
  waiting for transfers between devices  40.7 us (37%)
  starting transfers between devices  29.9 us (27%)
  Pallas kernels  25.5 us (23%)
  local copies, waits for them, and re-layouts  12.9 us (12%)
    ppermute x3, waiting for transfers between devices, body(): lax.ppermute(gate('piece', BEFORE_START if turn == 0 else ()), 'ch', PEER)  21.3 us
    pallas_call x3, Pallas kernels, project_peer(): pl.pallas_call(project_peer_kernel, out_shape=[jax.ShapeDtypeStruct((rows...  12.7 us
    ppermute x2, starting transfers between devices, body(): have[f'far{number}'] = lax.ppermute(together, 'ctx', ahead[1])  9.56 us
    all_to_all x1, waiting for transfers between devices, exchange_taps(): lax.all_to_all(copies, 'ctx', 0, 0, axis_index_groups=groups, tiled=True)  9.21 us
    pallas_call x1, Pallas kernels, project_own(): pl.pallas_call(project_own_kernel, out_shape=[jax.ShapeDtypeStruct((3, si...  8.92 us
    all_to_all x1, starting transfers between devices, exchange_taps(): lax.all_to_all(copies, 'ctx', 0, 0, axis_index_groups=groups, tiled=True)  7.44 us
    ppermute x2, starting transfers between devices, body(): have[f'near{number}'] = lax.ppermute(together, 'ctx', ahead[0])  6.54 us
    ppermute x2, waiting for transfers between devices, body(): have[f'near{number}'] = lax.ppermute(together, 'ctx', ahead[0])  5.95 us
  transfers between devices with their start and end apart: 13, of which 6 were waited for; matrix products, arithmetic and copies ran while one was open for 7% of the time, Pallas kernels for 20%

profile of v3, /device:TPU:64, one launch (start us, length us, event | category | flops | bytes accessed | tf_op | source)
XLA Modules:
  0.0 109.2 jit_solution(12571817931762588069)
XLA Ops:
  0.0 0.0 copy-start.5
  0.0 0.0 collective-permute-start
  0.0 3.3 %collective-permute-start.2 = (bf16[48,256]{1,0:T(8,128)(2,1)}, bf16[48,256]{1,0:T(8,128)(2,1)S(1)}, u32[]{:S(2)}, u32[]{:S(2)}) collective-permute-start(bf16[48,256]{1,0:T(8,128)(2,1)} %param.7), channel_id=1, source_target_pairs={{0,16},{4,20},{8,24},{12,28},{16,0},{20,4},{24,8},{28,12},{32,48},... | collective-permute-start | bytes 73736 | tf_op jit(solution)/shard_map/ppermute | solution.py:232
  3.3 0.0 copy-start.1
  3.3 2.7 %slice.10 = bf16[320,2048]{1,0:T(8,128)(2,1)} slice(bf16[768,2048]{1,0:T(8,128)(2,1)} %own), slice={[0:320], [0:2048]} | slice | bytes 2621440 | tf_op jit(solution)/shard_map/slice | solution.py:265
  6.0 0.0 collective-permute-done.2
  6.0 0.0 copy-done.5
  6.0 1.2 %collective-permute-start.3 = (bf16[320,2048]{1,0:T(8,128)(2,1)}, bf16[320,2048]{1,0:T(8,128)(2,1)}, u32[]{:S(2)}, u32[]{:S(2)}) collective-permute-start(bf16[320,2048]{1,0:T(8,128)(2,1)} %slice.10), channel_id=1, source_target_pairs={{0,2},{1,3},{2,0},{3,1},{4,6},{5,7},{6,4},{7,5},{8,10},{9,11},{10,... | collective-permute-start | bytes 3932168 | tf_op jit(solution)/shard_map/ppermute | solution.py:266
  7.3 0.9 broadcast_in_dim.2
  8.2 7.4 %all-to-all-start = ((bf16[16,2,48,256]{3,2,1,0:T(8,128)(2,1)}), bf16[16,2,48,256]{3,2,1,0:T(8,128)(2,1)}, u32[]{:S(2)}, u32[]{:S(2)}) async-start(bf16[16,2,48,256]{3,2,1,0:T(8,128)(2,1)} %broadcast_in_dim.2), calls=%async_computation | async-start | bytes 1572864 | tf_op jit(solution)/shard_map/all_to_all | solution.py:241
  15.7 0.0 collective-permute-done.sibling
  15.7 0.0 copy-done.1
  15.7 1.3 %slice.9 = bf16[384,2048]{1,0:T(8,128)(2,1)} slice(bf16[768,2048]{1,0:T(8,128)(2,1)S(1)} %copy-done.1), slice={[320:704], [0:2048]} | slice | bytes 3145728 | tf_op jit(solution)/shard_map/slice | solution.py:265
  17.0 0.0 copy-start.3
  17.0 0.9 collective-permute-start.1
  17.9 9.2 %all-to-all-done = bf16[16,2,48,256]{3,2,1,0:T(8,128)(2,1)} async-done(((bf16[16,2,48,256]{3,2,1,0:T(8,128)(2,1)}), bf16[16,2,48,256]{3,2,1,0:T(8,128)(2,1)}, u32[]{:S(2)}, u32[]{:S(2)}) %all-to-all-start) | async-done | bytes 786464 | tf_op jit(solution)/shard_map/all_to_all | solution.py:241
  27.1 2.1 %copy.6 = bf16[4,2,4,48,256]{4,3,2,1,0:T(8,128)(2,1)} copy(bf16[4,2,4,48,256]{4,3,1,2,0:T(8,128)(2,1)} %bitcast.7) | data formatting | bytes 1572864 | tf_op jit(solution)/shard_map/transpose | solution.py:242
  29.2 8.9 %collective-permute-done.3.peer = bf16[320,2048]{1,0:T(8,128)(2,1)} collective-permute-done((bf16[320,2048]{1,0:T(8,128)(2,1)}, bf16[320,2048]{1,0:T(8,128)(2,1)}, u32[]{:S(2)}, u32[]{:S(2)}) %collective-permute-start.3) | collective-permute-done | bytes 1310752 | tf_op jit(solution)/shard_map/ppermute | solution.py:266
  38.1 0.0 collective-permute-start.4
  38.1 0.1 pad_add_fusion.order
  38.1 0.0 copy-done.3
  38.1 0.0 copy-start.2
  38.1 1.1 %copy-done.2 = bf16[4,2,4,48,256]{4,3,2,1,0:T(8,128)(2,1)S(1)} copy-done((bf16[4,2,4,48,256]{4,3,2,1,0:T(8,128)(2,1)S(1)}, bf16[4,2,4,48,256]{4,3,2,1,0:T(8,128)(2,1)}, u32[]{:S(2)}) %copy-start.2) | copy-done | bytes 786456
  39.3 0.6 transform_taps.1.refs_10_
  39.9 0.0 copy-start
  39.9 4.6 %copy-done = bf16[8192,3,256]{2,0,1:T(8,128)(2,1)S(1)} copy-done((bf16[8192,3,256]{2,0,1:T(8,128)(2,1)S(1)}, bf16[8192,3,256]{2,0,1:T(8,128)(2,1)}, u32[]{:S(2)}) %copy-start) | copy-done | bytes 12582936
  44.4 8.9 %project_own.1 = (f32[3,320,256]{2,1,0:T(8,128)S(1)}, f32[3,384,256]{2,1,0:T(8,128)S(1)}, f32[3,64,256]{2,1,0:T(8,128)S(1)}) custom-call(s32[4]{0:T(128)S(1)} %pad_add_fusion.order, bf16[768,2048]{1,0:T(8,128)(2,1)S(1)} %copy-done.1, bf16[768,2048]{1,0:T(8,128)(2,1)} %collective-permute-done.sibling, bf16[3,8192,256]{2,1,0:T(8,128)(2,1)S(1)} %bitcast.11, ...), custom_call_target="tpu_custom_call" | custom-call | flops 1024 | bytes 1024 | tf_op jit(solution)/shard_map/project_own/pallas_call | solution.py:73
  53.4 0.0 collective-permute-done.4.peer_sibling
  53.4 5.2 %project_peer.3 = (bf16[320,256]{1,0:T(8,128)(2,1)S(1)}, bf16[320,256]{1,0:T(8,128)(2,1)S(1)}) custom-call(s32[4]{0:T(128)S(1)} %pad_add_fusion.order, bf16[320,2048]{1,0:T(8,128)(2,1)} %collective-permute-done.3.peer, bf16[320,2048]{1,0:T(8,128)(2,1)} %collective-permute-done.4.peer_sibling, f32[3,320,256]{2,1,0:T(8,128)S(1)} %get-tuple-element.33.known, ...), custom_call_target="tpu_custom_call" | custom-call | flops 1024 | bytes 1024 | tf_op jit(solution)/shard_map/project_peer/pallas_call | solution.py:117
  58.5 12.5 %collective-permute-done.1.peer = bf16[384,2048]{1,0:T(8,128)(2,1)} collective-permute-done((bf16[384,2048]{1,0:T(8,128)(2,1)}, bf16[384,2048]{1,0:T(8,128)(2,1)}, u32[]{:S(2)}, u32[]{:S(2)}) %collective-permute-start.1) | collective-permute-done | bytes 1572896 | tf_op jit(solution)/shard_map/ppermute | solution.py:266
  71.0 0.0 collective-permute-start.5
  71.0 0.9 collective-permute-start.7
  72.0 2.6 %collective-permute-done.5.peer_sibling = bf16[384,2048]{1,0:T(8,128)(2,1)S(1)} collective-permute-done((bf16[384,2048]{1,0:T(8,128)(2,1)}, bf16[384,2048]{1,0:T(8,128)(2,1)S(1)}, u32[]{:S(2)}, u32[]{:S(2)}) %collective-permute-start.5) | collective-permute-done | bytes 1572896 | tf_op jit(solution)/shard_map/ppermute | solution.py:274
  74.6 5.3 %project_peer.4 = (bf16[384,256]{1,0:T(8,128)(2,1)S(1)}, bf16[384,256]{1,0:T(8,128)(2,1)S(1)}) custom-call(s32[4]{0:T(128)S(1)} %pad_add_fusion.order, bf16[384,2048]{1,0:T(8,128)(2,1)} %collective-permute-done.1.peer, bf16[384,2048]{1,0:T(8,128)(2,1)S(1)} %collective-permute-done.5.peer_sibling, f32[3,384,256]{2,1,0:T(8,128)S(1)} %get-tuple-element.37.known, ...), custom_call_target="tpu_custom_call" | custom-call | flops 1024 | bytes 1024 | tf_op jit(solution)/shard_map/project_peer/pallas_call | solution.py:117
  79.9 3.4 %collective-permute-start.10 = (bf16[704,256]{1,0:T(8,128)(2,1)S(1)}, bf16[704,256]{1,0:T(8,128)(2,1)S(1)}, u32[]{:S(2)}, u32[]{:S(2)}) collective-permute-start(bf16[704,256]{1,0:T(8,128)(2,1)S(1)} %constant_dynamic-update-slice_fusion), channel_id=1, source_target_pairs={{0,4},{4,8},{8,12},{12,16},{16,20},{20,24},{24,28},{28,32},{32,36}... | collective-permute-start | bytes 1081352 | tf_op jit(solution)/shard_map/ppermute | solution.py:282
  83.3 4.6 %collective-permute-start.6 = (bf16[704,256]{1,0:T(8,128)(2,1)S(1)}, bf16[704,256]{1,0:T(8,128)(2,1)S(1)}, u32[]{:S(2)}, u32[]{:S(2)}) collective-permute-start(bf16[704,256]{1,0:T(8,128)(2,1)S(1)} %constant_dynamic-update-slice_fusion), channel_id=1, source_target_pairs={{0,8},{4,12},{8,16},{12,20},{16,24},{20,28},{24,32},{28,36},{32,40... | collective-permute-start | bytes 1081352 | tf_op jit(solution)/shard_map/ppermute | solution.py:283
  88.0 0.0 collective-permute-done.7.peer
  88.0 0.1 collective-permute-start.8
  88.1 1.5 %collective-permute-done.8.peer_sibling = bf16[64,2048]{1,0:T(8,128)(2,1)S(1)} collective-permute-done((bf16[64,2048]{1,0:T(8,128)(2,1)S(1)}, bf16[64,2048]{1,0:T(8,128)(2,1)S(1)}, u32[]{:S(2)}, u32[]{:S(2)}) %collective-permute-start.8) | collective-permute-done | bytes 262176 | tf_op jit(solution)/shard_map/ppermute | solution.py:274
  89.6 2.3 %project_peer.5 = (bf16[64,256]{1,0:T(8,128)(2,1)S(1)}, bf16[64,256]{1,0:T(8,128)(2,1)S(1)}) custom-call(s32[4]{0:T(128)S(1)} %pad_add_fusion.order, bf16[64,2048]{1,0:T(8,128)(2,1)S(1)} %collective-permute-done.7.peer, bf16[64,2048]{1,0:T(8,128)(2,1)S(1)} %collective-permute-done.8.peer_sibling, f32[3,64,256]{2,1,0:T(8,128)S(1)} %get-tuple-element.40.known, ...), custom_call_target="tpu_custom_call" | custom-call | flops 1024 | bytes 1024 | tf_op jit(solution)/shard_map/project_peer/pallas_call | solution.py:117
  91.9 3.1 %collective-permute-start.11 = (bf16[64,256]{1,0:T(8,128)(2,1)S(1)}, bf16[64,256]{1,0:T(8,128)(2,1)S(1)}, u32[]{:S(2)}, u32[]{:S(2)}) collective-permute-start(bf16[64,256]{1,0:T(8,128)(2,1)S(1)} %get-tuple-element.41.refs_6_), channel_id=1, source_target_pairs={{0,4},{4,8},{8,12},{12,16},{16,20},{20,24},{24,28},{28,32},{32,36}... | collective-permute-start | bytes 98312 | tf_op jit(solution)/shard_map/ppermute | solution.py:282
  95.0 4.9 %collective-permute-start.9 = (bf16[64,256]{1,0:T(8,128)(2,1)S(1)}, bf16[64,256]{1,0:T(8,128)(2,1)S(1)}, u32[]{:S(2)}, u32[]{:S(2)}) collective-permute-start(bf16[64,256]{1,0:T(8,128)(2,1)S(1)} %get-tuple-element.41.refs_6_), channel_id=1, source_target_pairs={{0,8},{4,12},{8,16},{12,20},{16,24},{20,28},{24,32},{28,36},{32,40... | collective-permute-start | bytes 98312 | tf_op jit(solution)/shard_map/ppermute | solution.py:283
  100.0 5.9 %collective-permute-done.11.refs_3_ = bf16[64,256]{1,0:T(8,128)(2,1)S(1)} collective-permute-done((bf16[64,256]{1,0:T(8,128)(2,1)S(1)}, bf16[64,256]{1,0:T(8,128)(2,1)S(1)}, u32[]{:S(2)}, u32[]{:S(2)}) %collective-permute-start.11) | collective-permute-done | bytes 32800 | tf_op jit(solution)/shard_map/ppermute | solution.py:282
  105.9 0.0 collective-permute-done.9.refs_1_
  105.9 0.0 collective-permute-done.10.refs_2_
  105.9 0.0 collective-permute-done.6.refs_0_
  105.9 0.0 copy-done.4
  105.9 3.3 %convolve.1 = bf16[768,256]{1,0:T(8,128)(2,1)} custom-call(bf16[704,256]{1,0:T(8,128)(2,1)S(1)} %collective-permute-done.6.refs_0_, bf16[64,256]{1,0:T(8,128)(2,1)S(1)} %collective-permute-done.9.refs_1_, bf16[704,256]{1,0:T(8,128)(2,1)S(1)} %collective-permute-done.10.refs_2_, bf16[64,256]{1,0:T(8,128)(2,1)S(1)} %collective-permute-done.11.refs_3_, ...), custom_call_target="tpu_custom_call" | custom-call | flops 1024 | bytes 1024 | tf_op jit(solution)/shard_map/convolve/pallas_call | solution.py:217
  (5 shorter events, 0.1 us)
Async XLA Ops:
  0.0 6.0 %copy-start.5 = (bf16[48,256]{1,0:T(8,128)(2,1)S(1)}, bf16[48,256]{1,0:T(8,128)(2,1)}, u32[]{:S(2)}) copy-start(bf16[48,256]{1,0:T(8,128)(2,1)} %param.7) | copy-start | bytes 73732
  0.0 15.7 %collective-permute-start = (bf16[768,2048]{1,0:T(8,128)(2,1)}, bf16[768,2048]{1,0:T(8,128)(2,1)}, u32[]{:S(2)}, u32[]{:S(2)}) collective-permute-start(bf16[768,2048]{1,0:T(8,128)(2,1)} %own), channel_id=1, source_target_pairs={{0,1},{1,0},{2,3},{3,2},{4,5},{5,4},{6,7},{7,6},{8,9},{9,8},{10,11... | collective-permute-start | bytes 9437192 | tf_op jit(solution)/shard_map/ppermute | solution.py:263
  0.0 6.0 %collective-permute-start.2 = (bf16[48,256]{1,0:T(8,128)(2,1)}, bf16[48,256]{1,0:T(8,128)(2,1)S(1)}, u32[]{:S(2)}, u32[]{:S(2)}) collective-permute-start(bf16[48,256]{1,0:T(8,128)(2,1)} %param.7), channel_id=1, source_target_pairs={{0,16},{4,20},{8,24},{12,28},{16,0},{20,4},{24,8},{28,12},{32,48},... | collective-permute-start | bytes 73736 | tf_op jit(solution)/shard_map/ppermute | solution.py:232
  3.3 12.4 %copy-start.1 = (bf16[768,2048]{1,0:T(8,128)(2,1)S(1)}, bf16[768,2048]{1,0:T(8,128)(2,1)}, u32[]{:S(2)}) copy-start(bf16[768,2048]{1,0:T(8,128)(2,1)} %own) | copy-start | bytes 9437188
  6.0 32.0 %collective-permute-start.3 = (bf16[320,2048]{1,0:T(8,128)(2,1)}, bf16[320,2048]{1,0:T(8,128)(2,1)}, u32[]{:S(2)}, u32[]{:S(2)}) collective-permute-start(bf16[320,2048]{1,0:T(8,128)(2,1)} %slice.10), channel_id=1, source_target_pairs={{0,2},{1,3},{2,0},{3,1},{4,6},{5,7},{6,4},{7,5},{8,10},{9,11},{10,... | collective-permute-start | bytes 3932168 | tf_op jit(solution)/shard_map/ppermute | solution.py:266
  8.2 18.9 %all-to-all-start = ((bf16[16,2,48,256]{3,2,1,0:T(8,128)(2,1)}), bf16[16,2,48,256]{3,2,1,0:T(8,128)(2,1)}, u32[]{:S(2)}, u32[]{:S(2)}) async-start(bf16[16,2,48,256]{3,2,1,0:T(8,128)(2,1)} %broadcast_in_dim.2), calls=%async_computation | async-start | bytes 1572864 | tf_op jit(solution)/shard_map/all_to_all | solution.py:241
  17.0 21.1 %copy-start.3 = (bf16[512,256]{1,0:T(8,128)(2,1)S(1)}, bf16[512,256]{1,0:T(8,128)(2,1)}, u32[]{:S(2)}) copy-start(bf16[512,256]{1,0:T(8,128)(2,1)} %constant.23.clone.forward.refs_11_) | copy-start | bytes 786436
  17.0 54.0 %collective-permute-start.1 = (bf16[384,2048]{1,0:T(8,128)(2,1)}, bf16[384,2048]{1,0:T(8,128)(2,1)}, u32[]{:S(2)}, u32[]{:S(2)}) collective-permute-start(bf16[384,2048]{1,0:T(8,128)(2,1)} %slice.9), channel_id=1, source_target_pairs={{0,2},{1,3},{2,0},{3,1},{4,6},{5,7},{6,4},{7,5},{8,10},{9,11},{10,... | collective-permute-start | bytes 4718600 | tf_op jit(solution)/shard_map/ppermute | solution.py:266
  38.1 15.3 %collective-permute-start.4 = (bf16[320,2048]{1,0:T(8,128)(2,1)}, bf16[320,2048]{1,0:T(8,128)(2,1)}, u32[]{:S(2)}, u32[]{:S(2)}) collective-permute-start(bf16[320,2048]{1,0:T(8,128)(2,1)} %collective-permute-done.3.peer), channel_id=1, source_target_pairs={{0,1},{1,0},{2,3},{3,2},{4,5},{5,4},{6,7},{7,6},{8,9},{9,8},{10,11... | collective-permute-start | bytes 3932168 | tf_op jit(solution)/shard_map/ppermute | solution.py:274
  38.1 1.1 %copy-start.2 = (bf16[4,2,4,48,256]{4,3,2,1,0:T(8,128)(2,1)S(1)}, bf16[4,2,4,48,256]{4,3,2,1,0:T(8,128)(2,1)}, u32[]{:S(2)}) copy-start(bf16[4,2,4,48,256]{4,3,2,1,0:T(8,128)(2,1)} %copy.6) | copy-start | bytes 2359300
  39.9 4.6 %copy-start = (bf16[8192,3,256]{2,0,1:T(8,128)(2,1)S(1)}, bf16[8192,3,256]{2,0,1:T(8,128)(2,1)}, u32[]{:S(2)}) copy-start(bf16[8192,3,256]{2,0,1:T(8,128)(2,1)} %param.6) | copy-start | bytes 37748740
  71.0 3.6 %collective-permute-start.5 = (bf16[384,2048]{1,0:T(8,128)(2,1)}, bf16[384,2048]{1,0:T(8,128)(2,1)S(1)}, u32[]{:S(2)}, u32[]{:S(2)}) collective-permute-start(bf16[384,2048]{1,0:T(8,128)(2,1)} %collective-permute-done.1.peer), channel_id=1, source_target_pairs={{0,1},{1,0},{2,3},{3,2},{4,5},{5,4},{6,7},{7,6},{8,9},{9,8},{10,11... | collective-permute-start | bytes 4718600 | tf_op jit(solution)/shard_map/ppermute | solution.py:274
  71.0 17.0 %collective-permute-start.7 = (bf16[64,2048]{1,0:T(8,128)(2,1)S(1)}, bf16[64,2048]{1,0:T(8,128)(2,1)S(1)}, u32[]{:S(2)}, u32[]{:S(2)}) collective-permute-start(bf16[64,2048]{1,0:T(8,128)(2,1)S(1)} %slice.11), channel_id=1, source_target_pairs={{0,2},{1,3},{2,0},{3,1},{4,6},{5,7},{6,4},{7,5},{8,10},{9,11},{10,... | collective-permute-start | bytes 786440 | tf_op jit(solution)/shard_map/ppermute | solution.py:266
  79.9 26.0 %collective-permute-start.10 = (bf16[704,256]{1,0:T(8,128)(2,1)S(1)}, bf16[704,256]{1,0:T(8,128)(2,1)S(1)}, u32[]{:S(2)}, u32[]{:S(2)}) collective-permute-start(bf16[704,256]{1,0:T(8,128)(2,1)S(1)} %constant_dynamic-update-slice_fusion), channel_id=1, source_target_pairs={{0,4},{4,8},{8,12},{12,16},{16,20},{20,24},{24,28},{28,32},{32,36}... | collective-permute-start | bytes 1081352 | tf_op jit(solution)/shard_map/ppermute | solution.py:282
  83.3 22.6 %collective-permute-start.6 = (bf16[704,256]{1,0:T(8,128)(2,1)S(1)}, bf16[704,256]{1,0:T(8,128)(2,1)S(1)}, u32[]{:S(2)}, u32[]{:S(2)}) collective-permute-start(bf16[704,256]{1,0:T(8,128)(2,1)S(1)} %constant_dynamic-update-slice_fusion), channel_id=1, source_target_pairs={{0,8},{4,12},{8,16},{12,20},{16,24},{20,28},{24,32},{28,36},{32,40... | collective-permute-start | bytes 1081352 | tf_op jit(solution)/shard_map/ppermute | solution.py:283
  88.0 1.6 %collective-permute-start.8 = (bf16[64,2048]{1,0:T(8,128)(2,1)S(1)}, bf16[64,2048]{1,0:T(8,128)(2,1)S(1)}, u32[]{:S(2)}, u32[]{:S(2)}) collective-permute-start(bf16[64,2048]{1,0:T(8,128)(2,1)S(1)} %collective-permute-done.7.peer), channel_id=1, source_target_pairs={{0,1},{1,0},{2,3},{3,2},{4,5},{5,4},{6,7},{7,6},{8,9},{9,8},{10,11... | collective-permute-start | bytes 786440 | tf_op jit(solution)/shard_map/ppermute | solution.py:274
  89.6 16.3 %copy-start.4 = (bf16[256,512]{1,0:T(8,128)(2,1)S(1)}, bf16[256,512]{1,0:T(8,128)(2,1)}, u32[]{:S(2)}) copy-start(bf16[256,512]{1,0:T(8,128)(2,1)} %constant.24.clone.refs_12_) | copy-start | bytes 786436
  91.9 14.0 %collective-permute-start.11 = (bf16[64,256]{1,0:T(8,128)(2,1)S(1)}, bf16[64,256]{1,0:T(8,128)(2,1)S(1)}, u32[]{:S(2)}, u32[]{:S(2)}) collective-permute-start(bf16[64,256]{1,0:T(8,128)(2,1)S(1)} %get-tuple-element.41.refs_6_), channel_id=1, source_target_pairs={{0,4},{4,8},{8,12},{12,16},{16,20},{20,24},{24,28},{28,32},{32,36}... | collective-permute-start | bytes 98312 | tf_op jit(solution)/shard_map/ppermute | solution.py:282
  95.0 10.9 %collective-permute-start.9 = (bf16[64,256]{1,0:T(8,128)(2,1)S(1)}, bf16[64,256]{1,0:T(8,128)(2,1)S(1)}, u32[]{:S(2)}, u32[]{:S(2)}) collective-permute-start(bf16[64,256]{1,0:T(8,128)(2,1)S(1)} %get-tuple-element.41.refs_6_), channel_id=1, source_target_pairs={{0,8},{4,12},{8,16},{12,20},{16,24},{20,28},{24,32},{28,36},{32,40... | collective-permute-start | bytes 98312 | tf_op jit(solution)/shard_map/ppermute | solution.py:283
